TPU v7x, 32 devices: a whole 2x2x4 slice. The times are simulated.
32 devices in a mesh: freq: 16 (over z, x, core), cuts: 2 (over y).
Axes of the slice: x: 2, y: 2, z: 4, core: 2. Of those that a mesh axis runs over, the one named last changes fastest.
Arguments:
- wavefield: bfloat16 [16, 2, 2048, 2048], P('freq', None, 'cuts'), may hold values from -6 to 6
- slowness: bfloat16 [16, 2048, 2048], P('freq', 'cuts'), may hold values from 0.25 to 0.546875
- block_inverse: bfloat16 [16, 2, 40, 64, 64], P('freq', None, 'cuts'), may hold values from -0.75 to 0.75
- block_lengths: int32 [16, 40], replicated, may hold values from 1 to 64, 2048 in all within a row
- slab_owner: int32 [1], replicated, may hold values from 0 to 15
- shot_position: int32 [2], replicated, may hold values from 0 to 2047
Outputs:
- image: float32 [1, 2048, 2048], P(None, 'cuts', 'freq')
Inputs may be any that keep to these rules, and one draw needn't show every extreme that they name: `block_lengths`: each row lists the lengths of the 40 blocks of a line in order; they sum to 2048 and the longest is exactly 64.
All inputs are finite; a program needn't handle non-finite values.
Results may differ from a plain program's by a relative error of at most 0.012.
Values may be sent and summed in bfloat16 or wider, within the bound.
A program may use at most 128 MiB of HBM per device.

v0:
```python
import math

import jax
import jax.numpy as jnp
from jax import lax
from jax.sharding import PartitionSpec as P

grid_step = 0.0125
depth_step = 0.02
slow_ref = 0.4
band_low = 5.0
band_width = 55.0


def spread(block, axis, owner):
    block = jnp.where(lax.axis_index(axis) == owner, block, jnp.zeros_like(block))
    return lax.psum(block, axis)


def split_length(extent):
    outer_len = 2 ** ((extent.bit_length() - 1) // 2)
    return (outer_len, extent // outer_len)


def outer_table(outer_len, orient):
    first_ids = jnp.arange(outer_len, dtype=jnp.int32)
    indices = first_ids[:, None] * first_ids[None, :] % outer_len
    angles = orient * 2.0 * math.pi / outer_len * indices.astype(jnp.float32)
    cosine = jnp.cos(angles) / math.sqrt(outer_len)
    sine = jnp.sin(angles) / math.sqrt(outer_len)
    first = jnp.stack([cosine, sine], axis=1)
    second = jnp.stack([-sine, cosine], axis=1)
    return jnp.stack([first, second], axis=0).astype(jnp.bfloat16)


def inner_table(outer_len, inner_len, orient):
    extent = outer_len * inner_len
    outer_ids = jnp.arange(outer_len, dtype=jnp.int32)[:, None, None]
    inner_ids = jnp.arange(inner_len, dtype=jnp.int32)[None, :, None]
    freq_ids = jnp.arange(inner_len, dtype=jnp.int32)[None, None, :]
    indices = inner_ids * (outer_ids + outer_len * freq_ids) % extent
    angles = orient * 2.0 * math.pi / extent * indices.astype(jnp.float32)
    cosine = jnp.cos(angles) / math.sqrt(inner_len)
    sine = jnp.sin(angles) / math.sqrt(inner_len)
    first = jnp.stack([cosine, sine], axis=2)
    second = jnp.stack([-sine, cosine], axis=2)
    return jnp.stack([first, second], axis=2).astype(jnp.bfloat16)


def mixing(formula, operand, table):
    return jnp.einsum(formula, operand, table, preferred_element_type=jnp.float32)


def forward_lines(field):
    rows = field.shape[1]
    outer_len, inner_len = split_length(field.shape[2])
    shaped = field.reshape(2, rows, outer_len, inner_len)
    first_section = mixing("cmab,cadk->mbdk", shaped, outer_table(outer_len, -1.0)).astype(
        jnp.bfloat16
    )
    return mixing(
        "mbdk,kbdeq->kmeq", first_section, inner_table(outer_len, inner_len, -1.0)
    ).astype(jnp.bfloat16)


def across_forward(columns):
    count_k, extent_x, _, count_q = columns.shape
    outer_len, inner_len = split_length(extent_x)
    shaped = columns.reshape(count_k, outer_len, inner_len, 2, count_q)
    first_section = mixing("kabcq,cadz->kbqdz", shaped, outer_table(outer_len, -1.0)).astype(
        jnp.bfloat16
    )
    return mixing("kbqdz,zbdwu->zkqwu", first_section, inner_table(outer_len, inner_len, -1.0))


def across_inverse(spectrum, extent_x):
    count_k = spectrum.shape[1]
    count_q = spectrum.shape[2]
    outer_len, inner_len = split_length(extent_x)
    first_section = mixing(
        "zkqwu,zbwdu->zkqdb", spectrum, inner_table(outer_len, inner_len, 1.0)
    ).astype(jnp.bfloat16)
    second_section = mixing("zkqdb,daez->kabeq", first_section, outer_table(outer_len, 1.0)).astype(
        jnp.bfloat16
    )
    return second_section.reshape(count_k, extent_x, 2, count_q)


def lines_inverse(spectrum, extent_y):
    rows = spectrum.shape[1]
    outer_len, inner_len = split_length(extent_y)
    first_section = mixing(
        "kmdq,kbdeq->kmeb", spectrum, inner_table(outer_len, inner_len, 1.0)
    ).astype(jnp.bfloat16)
    second_section = mixing("kmeb,eack->cmab", first_section, outer_table(outer_len, 1.0))
    return second_section.reshape(2, rows, extent_y)


def wave_numbers(indices, extent):
    signed = jnp.where(indices < extent // 2, indices, indices - extent)
    return signed.astype(jnp.float32) * (2.0 * math.pi / (extent * grid_step))


def propagator(angular, k_start, k_count, extent_x, extent_y):
    outer_x, inner_x = split_length(extent_x)
    outer_y, inner_y = split_length(extent_y)
    cross_ids = (
        jnp.arange(outer_x, dtype=jnp.int32)[:, None]
        + outer_x * jnp.arange(inner_x, dtype=jnp.int32)[None, :]
    )
    line_ids = (k_start + jnp.arange(k_count, dtype=jnp.int32))[:, None] + outer_y * jnp.arange(
        inner_y, dtype=jnp.int32
    )[None, :]
    wave_x = wave_numbers(cross_ids, extent_x)
    wave_y = wave_numbers(line_ids, extent_y)
    vertical = (
        (angular * slow_ref) ** 2 - wave_x[:, None, None, :] ** 2 - wave_y[None, :, :, None] ** 2
    )
    root_abs = jnp.sqrt(jnp.abs(vertical))
    real_part = jnp.where(
        vertical > 0, jnp.cos(root_abs * depth_step), jnp.exp(-root_abs * depth_step)
    )
    imag_part = jnp.where(vertical > 0, jnp.sin(root_abs * depth_step), jnp.zeros_like(root_abs))
    return (real_part, imag_part)


def shift_phase(kspace, prop_re, prop_im):
    real_in = kspace[:, :, :, 0, :]
    imag_in = kspace[:, :, :, 1, :]
    real_out = real_in * prop_re - imag_in * prop_im
    imag_out = real_in * prop_im + imag_in * prop_re
    return jnp.stack([real_out, imag_out], axis=3).astype(jnp.bfloat16)


def block_correction(turned, matrices, block_len, extent_y):
    block_count = matrices.shape[1]
    capacity = matrices.shape[2]
    starts = jnp.cumsum(block_len) - block_len
    offsets = jnp.arange(capacity, dtype=jnp.int32)
    source = jnp.minimum(starts[:, None] + offsets[None, :], extent_y - 1).reshape(-1)
    occupied = (offsets[None, :] < block_len[:, None]).reshape(-1)

    def slotted(part):
        picked = jnp.take(part, source, axis=1)
        picked = jnp.where(occupied[None, :], picked, jnp.zeros_like(picked))
        return picked.reshape(part.shape[0], block_count, capacity)

    slot_re = slotted(turned[0])
    slot_im = slotted(turned[1])

    def product(first_op, second_op):
        return jnp.einsum("rcj,cij->rci", first_op, second_op, preferred_element_type=jnp.float32)

    out_re = product(slot_re, matrices[0]) - product(slot_im, matrices[1])
    out_im = product(slot_re, matrices[1]) + product(slot_im, matrices[0])
    cell_ids = jnp.arange(extent_y, dtype=jnp.int32)
    block_end = starts + block_len
    shift_sum = jnp.sum(
        jnp.where(block_end[None, :] <= cell_ids[:, None], capacity - block_len[None, :], 0), axis=1
    )
    position = cell_ids + shift_sum
    back_re = jnp.take(out_re.reshape(out_re.shape[0], -1), position, axis=1)
    back_im = jnp.take(out_im.reshape(out_im.shape[0], -1), position, axis=1)
    return (back_re, back_im)


def image_phase(angular, rows_x, cols_y, shot_position, depth_index):
    offset_x = (rows_x - shot_position[0]).astype(jnp.float32) * grid_step
    offset_y = (cols_y - shot_position[1]).astype(jnp.float32) * grid_step
    depth_now = (depth_index + 1) * depth_step
    distance = jnp.sqrt(offset_x[:, None] ** 2 + offset_y[None, :] ** 2 + depth_now * depth_now)
    return angular * slow_ref * distance


def body(wavefield, slowness, block_inverse, block_lengths, slab_owner, shot_position):
    cut_count = lax.axis_size("cuts")
    freq_total = lax.axis_size("freq")
    row_count = wavefield.shape[2]
    extent_y = wavefield.shape[3]
    extent_x = row_count * cut_count
    outer_y, inner_y = split_length(extent_y)
    local_k = outer_y // cut_count
    freq_index = lax.axis_index("freq")
    cut_index = lax.axis_index("cuts")
    angular = (
        2.0
        * math.pi
        * (band_low + band_width * (freq_index.astype(jnp.float32) + 0.5) / freq_total)
    )
    prop_re, prop_im = propagator(angular, cut_index * local_k, local_k, extent_x, extent_y)
    rows_x = cut_index * row_count + jnp.arange(row_count, dtype=jnp.int32)
    cols_y = jnp.arange(extent_y, dtype=jnp.int32)
    whole_blocks = lax.all_gather(block_inverse, "cuts", axis=2, tiled=True)
    current = wavefield[0]
    spectrum = forward_lines(current)
    columns = lax.all_to_all(spectrum, "cuts", split_axis=0, concat_axis=1, tiled=True)
    kspace = across_forward(columns)
    shifted = shift_phase(kspace, prop_re, prop_im)
    restored = across_inverse(shifted, extent_x)
    row_field = lax.all_to_all(restored, "cuts", split_axis=1, concat_axis=0, tiled=True)
    spatial = lines_inverse(row_field, extent_y)
    owner_id = slab_owner[0]
    slab_now = spread(slowness, "freq", owner_id)
    matrices = spread(whole_blocks, "freq", owner_id)
    block_len = lax.dynamic_index_in_dim(block_lengths, owner_id, 0, keepdims=False)
    slab_now, matrices, block_len = (slab_now[0], matrices[0], block_len)
    phases = angular * depth_step * (slab_now.astype(jnp.float32) - slow_ref)
    cos_part = jnp.cos(phases)
    sin_part = jnp.sin(phases)
    turned = (
        (spatial[0] * cos_part - spatial[1] * sin_part).astype(jnp.bfloat16),
        (spatial[0] * sin_part + spatial[1] * cos_part).astype(jnp.bfloat16),
    )
    correction = block_correction(turned, matrices, block_len, extent_y)
    values_re = turned[0].astype(jnp.float32) + correction[0]
    values_im = turned[1].astype(jnp.float32) + correction[1]
    angle_img = image_phase(angular, rows_x, cols_y, shot_position, 0)
    image_part = (values_re * jnp.cos(angle_img) - values_im * jnp.sin(angle_img)) * (
        1.0 / math.sqrt(freq_total)
    )
    images = [lax.psum_scatter(image_part, "freq", scatter_dimension=1, tiled=True)]
    return jnp.stack(images)


def solution(mesh):
    placed = (
        P("freq", None, "cuts", None),
        P("freq", "cuts", None),
        P("freq", None, "cuts", None, None),
        P(),
        P(),
        P(),
    )
    return jax.shard_map(
        body, mesh=mesh, in_specs=placed, out_specs=P(None, "cuts", "freq"), check_vma=False
    )
```

profile of v0, /device:TPU:0, one launch (start us, length us, event | category | flops | bytes accessed | tf_op | source)
XLA Modules:
  0.0 951.1 jit_solution(812893936782377530)
XLA Ops:
  16.3 11.9 %copy.71 = bf16[1,2,1024,2048]{2,3,1,0:T(8,128)(2,1)} copy(bf16[1,2,1024,2048]{3,2,1,0:T(8,128)(2,1)} %param.10) | data formatting | bytes 16777216 | tf_op args[0]
  29.9 14.6 %fusion.33 = bf16[1024,64,2,32,1]{0,3,1,2,4:T(8,128)(2,1)S(1)} fusion(bf16[2,1024,32,64]{1,3,2,0:T(8,128)(2,1)} %bitcast.222, bf16[1,32,2,32]{1,3,0,2:T(8,128)(2,1)S(1)} %get-tuple-element.34, bf16[1,32,2,32]{1,3,0,2:T(8,128)(2,1)S(1)} %get-tuple-element.33), kind=kOutput, calls=%fused_computation.40 | convolution fusion | flops 541081600 | bytes 16785408 | tf_op jit(solution)/shard_map/cmab,cadk->mbdk/dot_general | solution.py:51
  44.6 13.3 %bitcast_convert_fusion.4 = bf16[32,1024,2,64]{1,3,2,0:T(8,128)(2,1)} fusion(bf16[1024,64,2,32,1]{0,3,1,2,4:T(8,128)(2,1)S(1)} %fusion.33, bf16[32,64,1,2,64]{1,4,2,3,0:T(8,128)(2,1)S(1)} %get-tuple-element.22, bf16[32,64,1,2,64]{1,4,2,3,0:T(8,128)(2,1)S(1)} %get-tuple-element.21), kind=kOutput, calls=%fused_computation.36 | convolution fusion | flops 1080033280 | bytes 17825792 | tf_op jit(solution)/shard_map/mbdk,kbdeq->kmeq/dot_general | solution.py:51
  67.4 91.3 %all-to-all-done = bf16[32,1024,2,64]{1,3,2,0:T(8,128)(2,1)} async-done(((bf16[32,1024,2,64]{1,3,2,0:T(8,128)(2,1)}), bf16[32,1024,2,64]{1,3,2,0:T(8,128)(2,1)}, u32[]{:S(2)}, u32[]{:S(2)}) %all-to-all-start) | async-done | bytes 8388640 | tf_op jit(solution)/shard_map/all_to_all | solution.py:196
  158.7 16.7 %copy.168 = bf16[2,16,1024,2,64]{2,0,4,3,1:T(2,128)(2,1)} copy(bf16[2,16,1024,2,64]{2,4,3,1,0:T(8,128)(2,1)} %bitcast.23) | data formatting | bytes 16777216 | tf_op jit(solution)/shard_map/all_to_all | solution.py:196
  175.3 26.6 %reshape.441 = bf16[16,32,64,2,64]{2,1,4,3,0:T(8,128)(2,1)} reshape(bf16[16,2,1024,2,64]{2,1,4,3,0:T(2,128)(2,1)} %bitcast.221) | data formatting | bytes 16777216 | tf_op jit(solution)/shard_map/reshape | solution.py:69
  213.4 22.4 %fusion.25 = f32[32,16,64,2,64]{4,2,3,1,0:T(8,128)} fusion(bf16[16,64,64,2,32,1]{1,4,3,2,0,5:T(8,128)(2,1)} %fusion.15, bf16[32,64,1,2,64]{1,4,2,3,0:T(8,128)(2,1)} %copy-done.2, bf16[32,64,1,2,64]{1,4,2,3,0:T(8,128)(2,1)S(1)} %get-tuple-element.21), kind=kOutput, calls=%fused_computation.38 | convolution fusion | flops 1075838976 | bytes 26214400 | tf_op jit(solution)/shard_map/kbqdz,zbdwu->zkqwu/dot_general | solution.py:51
  235.8 76.5 %fusion.10 = (bf16[32,16,64,1,64]{4,2,3,1,0:T(8,128)(2,1)S(1)}, bf16[32,16,64,1,64]{4,2,3,1,0:T(8,128)(2,1)}) fusion(f32[32,16,64,2,64]{4,2,3,1,0:T(8,128)} %fusion.25, f32[16,64]{1,0:T(8,128)S(1)} %fusion.89, f32[32,64]{1,0:T(8,128)S(1)} %fusion.81), kind=kLoop, calls=%fused_computation.19 | loop fusion | flops 33554432 | bytes 25178112 | tf_op jit(solution)/shard_map/convert
  312.4 13.6 %fusion.16 = bf16[32,16,64,2,64]{2,4,1,3,0:T(8,128)(2,1)} fusion(bf16[32,16,64,1,64]{4,2,3,1,0:T(8,128)(2,1)} %get-tuple-element.12, bf16[32,16,64,1,64]{4,2,3,1,0:T(8,128)(2,1)S(1)} %get-tuple-element.11, bf16[32,64,2,2,64,1]{1,4,3,0,2,5:T(8,128)(2,1)S(1)} %copy-done.3), kind=kOutput, calls=%fused_computation.25 | convolution fusion | flops 1094713344 | bytes 17825792 | tf_op jit(solution)/shard_map/zkqwu,zbwdu->zkqdb/dot_general | solution.py:51
  325.9 25.0 %copy.81 = bf16[32,16,64,2,64]{4,0,3,2,1:T(8,128)(2,1)} copy(bf16[32,16,64,2,64]{2,4,1,3,0:T(8,128)(2,1)} %fusion.16) | data formatting | bytes 16777216 | tf_op jit(solution)/shard_map/convert_element_type | solution.py:82
  350.9 13.9 %fusion.28 = bf16[16,32,64,2,64]{2,1,4,0,3:T(8,128)(2,1)} fusion(bf16[32,16,64,2,64]{4,0,3,2,1:T(8,128)(2,1)} %copy.81, bf16[2,32,2,32,1,1]{1,3,2,0,5,4:T(8,128)(2,1)S(1)} %get-tuple-element.24), kind=kOutput, calls=%fused_computation.39 | convolution fusion | flops 541065216 | bytes 16785408 | tf_op jit(solution)/shard_map/zkqdb,daez->kabeq/dot_general | solution.py:51
  364.8 45.7 %copy.129 = bf16[16,32,64,2,64]{4,3,0,2,1:T(2,128)(2,1)} copy(bf16[16,32,64,2,64]{2,1,4,0,3:T(8,128)(2,1)} %fusion.28) | data formatting | bytes 16777216 | tf_op jit(solution)/shard_map/reshape | solution.py:86
  410.5 23.9 %reshape.516 = bf16[2,2,1048576]{2,1,0:T(2,128)(2,1)} reshape(bf16[2048,16,2,64]{3,2,1,0:T(2,128)(2,1)} %bitcast.217) | data formatting | bytes 16777216
  448.5 98.8 %all_gather.3 = bf16[1,2,40,64,64]{4,3,2,1,0:T(8,128)(2,1)S(1)} all-gather(bf16[1,2,20,64,64]{4,3,2,1,0:T(8,128)(2,1)S(1)} %copy-done.4), channel_id=1, replica_groups=mesh['freq'=16,'cuts'=2] {'cuts'}, dimensions={2}, use_global_device_ids=true | all-gather | bytes 983040 | tf_op jit(solution)/shard_map/all_gather | solution.py:193
  556.0 23.7 %reshape.517 = bf16[2048,16,2,64]{3,2,1,0:T(2,128)(2,1)} reshape(bf16[2,2,1048576]{2,1,0:T(2,128)(2,1)} %all-to-all-done.1) | data formatting | bytes 16777216
  579.7 39.1 %copy.132 = bf16[2,16,1024,2,64]{2,4,1,0,3:T(8,128)(2,1)} copy(bf16[2,16,1024,2,64]{4,3,1,2,0:T(2,128)(2,1)} %bitcast.216) | data formatting | bytes 16777216 | tf_op jit(solution)/shard_map/all_to_all | solution.py:200
  636.6 15.2 %fusion.52 = f32[2,1024,32,64]{1,2,3,0:T(8,128)S(1)} fusion(bf16[32,1024,2,64]{1,3,2,0:T(8,128)(2,1)} %bitcast.223, bf16[2,32,2,32,1]{1,3,2,0,4:T(8,128)(2,1)S(1)} %get-tuple-element.23), kind=kOutput, calls=%fused_computation.67 | convolution fusion | flops 536870912 | bytes 25174016 | tf_op jit(solution)/shard_map/kmeb,eack->cmab/dot_general | solution.py:51
  679.2 34.6 %fusion.42 = (bf16[1024,2048]{0,1:T(8,128)(2,1)}, bf16[1024,2048]{0,1:T(8,128)(2,1)}) fusion(f32[1,1024,32,64]{1,3,2,0:T(8,128)} %copy.91, f32[1,1024,32,64]{1,3,2,0:T(8,128)} %copy.89, bf16[1,1024,2048]{1,2,0:T(8,128)(2,1)} %get-tuple-element.6, f32[]{:T(128)S(6)} %mul.496), kind=kLoop, calls=%fused_computation.53 | loop fusion | flops 23068672 | bytes 29360132 | tf_op jit(solution)/shard_map/convert_element_type | solution.py:212
  713.8 15.0 %gather_fusion = bf16[2560,1024]{1,0:T(8,128)(2,1)} fusion(bf16[1024,2048]{0,1:T(8,128)(2,1)} %get-tuple-element.14, s32[3072]{0:T(1024)S(1)} %pad_clamp_fusion), kind=kCustom, calls=%fused_computation.clone | custom fusion | bytes 10496000 | tf_op jit(solution)/shard_map/jit(_take)/gather | solution.py:144
  728.8 14.8 %gather_fusion.1 = bf16[2560,1024]{1,0:T(8,128)(2,1)} fusion(bf16[1024,2048]{0,1:T(8,128)(2,1)} %get-tuple-element.13, s32[3072]{0:T(1024)S(1)} %pad_clamp_fusion), kind=kCustom, calls=%fused_computation.2.clone | custom fusion | bytes 10496000 | tf_op jit(solution)/shard_map/jit(_take)/gather | solution.py:144
  765.6 15.7 %gather_fusion.2 = f32[2048,1024]{1,0:T(8,128)} fusion(f32[1024,2560]{0,1:T(8,128)} %bitcast.213, s32[2048]{0:T(1024)S(1)} %fusion.90), kind=kCustom, calls=%fused_computation.1.clone | custom fusion | bytes 16785408 | tf_op jit(solution)/shard_map/jit(_take)/gather | solution.py:162
  781.3 15.7 %gather_fusion.3 = f32[2048,1024]{1,0:T(8,128)} fusion(f32[1024,2560]{0,1:T(8,128)} %bitcast.212, s32[2048]{0:T(1024)S(1)} %fusion.90), kind=kCustom, calls=%fused_computation.3.clone | custom fusion | bytes 16785408 | tf_op jit(solution)/shard_map/jit(_take)/gather | solution.py:163
  797.0 40.2 %fusion.37 = f32[1024,2048]{0,1:T(8,128)} fusion(f32[2048,1024]{1,0:T(8,128)} %gather_fusion.3, f32[2048,1024]{1,0:T(8,128)} %gather_fusion.2, bf16[1024,2048]{0,1:T(8,128)(2,1)} %get-tuple-element.13, bf16[1024,2048]{0,1:T(8,128)(2,1)} %get-tuple-element.14, f32[2048]{0:T(1024)S(1)} %copy-done.5, f32[1024]{0:T(1024)S(1)} %copy-done.6, f32[]{:T(128)S(6)} %mul.503, ...), kind=kLoop, calls=%fused_computation.45 | loop fusion | flops 27262976 | bytes 33568772 | tf_op jit(solution)/shard_map/mul | solution.py:218
  837.3 104.8 %reduce-scatter.2.cloned.1.call-done = f32[1024,128]{0,1:T(8,128)} async-done(((f32[1024,2048]{0,1:T(8,128)}), f32[1024,128]{0,1:T(8,128)}) %reduce-scatter.2.cloned.1.call-update) | async-done | bytes 524304 | tf_op jit(solution)/shard_map/reduce_scatter | solution.py:221
  (75 shorter events, 123.6 us)
Async XLA Ops:
  29.9 14.7 %copy-start.2 = (bf16[32,64,1,2,64]{1,4,2,3,0:T(8,128)(2,1)}, bf16[32,64,1,2,64]{1,4,2,3,0:T(8,128)(2,1)S(1)}, u32[]{:S(2)}) copy-start(bf16[32,64,1,2,64]{1,4,2,3,0:T(8,128)(2,1)S(1)} %get-tuple-element.22) | copy-start | bytes 1572868
  57.8 100.8 %all-to-all-start = ((bf16[32,1024,2,64]{1,3,2,0:T(8,128)(2,1)}), bf16[32,1024,2,64]{1,3,2,0:T(8,128)(2,1)}, u32[]{:S(2)}, u32[]{:S(2)}) async-start(bf16[32,1024,2,64]{1,3,2,0:T(8,128)(2,1)} %bitcast_convert_fusion.4), calls=%async_computation | async-start | bytes 16777216 | tf_op jit(solution)/shard_map/all_to_all | solution.py:196
  235.8 76.5 %copy-start.3 = (bf16[32,64,2,2,64,1]{1,4,3,0,2,5:T(8,128)(2,1)S(1)}, bf16[32,64,2,2,64,1]{1,4,3,0,2,5:T(8,128)(2,1)}, u32[]{:S(2)}) copy-start(bf16[32,64,2,2,64,1]{1,4,3,0,2,5:T(8,128)(2,1)} %get-tuple-element.18) | copy-start | bytes 3145732
  434.4 121.6 %all-to-all-start.1 = ((bf16[2,2,1048576]{2,1,0:T(2,128)(2,1)}), bf16[2,2,1048576]{2,1,0:T(2,128)(2,1)}, u32[]{:S(2)}, u32[]{:S(2)}) async-start(bf16[2,2,1048576]{2,1,0:T(2,128)(2,1)} %reshape.516), calls=%async_computation.1 | async-start | bytes 16777216 | tf_op jit(solution)/shard_map/all_to_all | solution.py:200
  441.4 7.2 copy-start.4
  441.4 237.9 %all-reduce.3.cloned.1.call-start = ((), (), s32[]{:S(2)}) async-start(), calls=%async_computation.4 | async-start | bytes 11010048 | tf_op jit(solution)/shard_map/psum | solution.py:17
  547.3 4.7 copy-start.8
  550.7 391.4 %reduce-scatter.2.cloned.1.call-start = ((), (), s32[]{:S(2)}) async-start(), calls=%async_computation.3 | async-start | bytes 8912896 | tf_op jit(solution)/shard_map/reduce_scatter | solution.py:221
  659.0 11.7 %copy-start = (f32[1,1024,32,64]{1,2,3,0:T(8,128)S(1)}, f32[1,1024,32,64]{1,2,3,0:T(8,128)}, u32[]{:S(2)}) copy-start(f32[1,1024,32,64]{1,2,3,0:T(8,128)} %get-tuple-element.16) | copy-start | bytes 25165828
  743.6 5.9 copy-start.1
  781.3 15.7 %copy-start.5 = (f32[2048]{0:T(1024)S(1)}, f32[2048]{0:T(1024)}, u32[]{:S(2)}) copy-start(f32[2048]{0:T(1024)} %multiply_multiply_fusion) | copy-start | bytes 24580
  781.3 15.7 %copy-start.6 = (f32[1024]{0:T(1024)S(1)}, f32[1024]{0:T(1024)}, u32[]{:S(2)}) copy-start(f32[1024]{0:T(1024)} %multiply_multiply_fusion.1) | copy-start | bytes 12292
  781.3 15.7 %copy-start.7 = (pred[2048]{0:T(1024)(128)(4,1)S(1)}, pred[2048]{0:T(1024)(128)(4,1)}, u32[]{:S(2)}) copy-start(pred[2048]{0:T(1024)(128)(4,1)} %compare_and_fusion.1) | copy-start | bytes 6148
Sparse Core Ops, SparseCore 0:
  550.8 128.3 all-reduce.2
  837.4 104.6 reduce-scatter.1
where the time goes:
time: 965 us; the launch traced here: 951 us
  local copies, waits for them, and re-layouts  319 us (33%)
  waiting for transfers between devices  197 us (20%)
  other arithmetic  179 us (19%)
  matrix products  130 us (13%)
  blocking collectives  98.8 us (10%)
  between operations  14.5 us (2%)
  starting transfers between devices  14 us (1%)
    dot_general x8, matrix products, mixing(): jnp.einsum(formula, operand, table, preferred_element_type=jnp.float32)  114 us
    reduce_scatter x1, waiting for transfers between devices, body(): lax.psum_scatter(image_part, 'freq', scatter_dimension=1, tiled=True)  105 us
    all_gather x1, blocking collectives, body(): whole_blocks = lax.all_gather(block_inverse, 'cuts', axis=2, tiled=True)  98.8 us
    all_to_all x1, waiting for transfers between devices, body(): lax.all_to_all(spectrum, 'cuts', split_axis=0, concat_axis=1, tiled=True)  91.3 us
    another operation x8, other arithmetic  86.6 us
    unnamed x22, local copies, waits for them, and re-layouts  65.9 us
    reshape x1, local copies, waits for them, and re-layouts, across_inverse(): return second_section.reshape(count_k, extent_x, 2, count_q)  45.7 us
    mul x1, other arithmetic, body(): (values_re * jnp.cos(angle_img) - values_im * jnp.sin(angle_img)) * (1.0...  40.2 us
  transfers between devices with their start and end apart: 4, of which 3 were waited for; matrix products, arithmetic and copies ran while one was open for 15% of the time, Pallas kernels for 0%

commit v1 on v0

v1 whole, which is shorter than its diff:
```python
import functools
import math

import jax
import jax.numpy as jnp
import numpy as np
from jax import lax
from jax.experimental import pallas as pl
from jax.experimental.pallas import tpu as pltpu
from jax.sharding import PartitionSpec as P

grid_step = 0.0125
depth_step = 0.02
slow_ref = 0.4
band_low = 5.0
band_width = 55.0

RADIX = 8
SUB = 16
LANE = 128
PAD = 128
VMEM_LIMIT = 56 * 1024 * 1024
BF = jnp.bfloat16
F32 = jnp.float32


def fit(fn, top, degree):
    cheb = np.polynomial.chebyshev.Chebyshev.interpolate(fn, degree, domain=[0.0, top])
    return [float(c) for c in cheb.convert(kind=np.polynomial.Polynomial).coef]


def root_cos(w):
    return np.cos(np.sqrt(np.maximum(w, 0.0)))


def root_sinc(w):
    return np.sinc(np.sqrt(np.maximum(w, 0.0)) / np.pi)


COS_WIDE = fit(root_cos, 10.0, 7)
SINC_WIDE = fit(root_sinc, 10.0, 6)
COS_SLIM = fit(root_cos, 1.6, 4)
SINC_SLIM = fit(root_sinc, 1.6, 4)


def horner(coefs, x):
    acc = jnp.full_like(x, coefs[-1])
    for c in coefs[-2::-1]:
        acc = acc * x + c
    return acc


def fourier_tables(extent):
    inner = extent // RADIX
    k = np.arange(RADIX)[:, None, None]
    q = np.arange(inner)[None, :, None]
    b = np.arange(inner)[None, None, :]
    angle = 2.0 * np.pi / extent * ((b * (k + RADIX * q)) % extent)
    cosine = np.cos(angle) / math.sqrt(extent)
    sine = np.sin(angle) / math.sqrt(extent)
    top = np.concatenate([cosine, sine], axis=2)
    low = np.concatenate([-sine, cosine], axis=2)
    table = np.concatenate([top, low], axis=1).astype(np.float32)
    return table.astype(BF), np.ascontiguousarray(table.transpose(0, 2, 1)).astype(BF)


def radix8(parts, sign):
    def add(x, y):
        return (x[0] + y[0], x[1] + y[1])

    def sub(x, y):
        return (x[0] - y[0], x[1] - y[1])

    def turn(x):
        return (x[1], -x[0]) if sign < 0 else (-x[1], x[0])

    half = math.sqrt(0.5)

    def four(x0, x1, x2, x3):
        t0, t1, t2, t3 = add(x0, x2), sub(x0, x2), add(x1, x3), turn(sub(x1, x3))
        return [add(t0, t2), add(t1, t3), sub(t0, t2), sub(t1, t3)]

    even = four(parts[0], parts[2], parts[4], parts[6])
    odd = four(parts[1], parts[3], parts[5], parts[7])
    turned1 = turn(odd[1])
    turned3 = turn(odd[3])
    odd[1] = ((odd[1][0] + turned1[0]) * half, (odd[1][1] + turned1[1]) * half)
    odd[2] = turn(odd[2])
    odd[3] = ((turned3[0] - odd[3][0]) * half, (turned3[1] - odd[3][1]) * half)
    return [add(even[i], odd[i]) for i in range(4)] + [sub(even[i], odd[i]) for i in range(4)]


def rows_of(step):
    return pl.ds(pl.multiple_of(step * SUB, SUB), SUB)


def residue(cut, shift, chunk, cuts, per):
    return lax.rem(cut + (cuts - shift), cuts) * per + chunk


def lines_kernel(cuts, cut_ref, p_ref, ft_ref, *rest):
    outs, y1 = rest[:-1], rest[-1]
    rows, extent = p_ref.shape[1], p_ref.shape[2]
    inner = extent // RADIX
    per = RADIX // cuts

    @pl.loop(0, rows // SUB)
    def _(step):
        at = rows_of(step)
        for l in range(0, inner, LANE):
            parts = [
                (
                    p_ref[0, at, a * inner + l : a * inner + l + LANE].astype(F32),
                    p_ref[1, at, a * inner + l : a * inner + l + LANE].astype(F32),
                )
                for a in range(RADIX)
            ]
            for k, (re, im) in enumerate(radix8(parts, -1)):
                y1[k, at, l : l + LANE] = re.astype(BF)
                y1[k, at, inner + l : inner + l + LANE] = im.astype(BF)

    cut = cut_ref[0]
    for s in range(cuts):
        for c in range(per):
            k = residue(cut, s, c, cuts, per)
            outs[s * per + c][...] = jnp.dot(y1[k], ft_ref[k], preferred_element_type=F32).astype(BF)


def across_kernel(cuts, *refs):
    pieces = refs[:cuts]
    f_ref, ft_ref, wx_ref, wy_ref = refs[cuts : cuts + 4]
    outs = refs[cuts + 4 : -3]
    y1, z, kb = refs[-3:]
    rows = pieces[0].shape[0]
    inner = rows * cuts // RADIX
    width = pieces[0].shape[1] // 2

    @pl.loop(0, inner // SUB)
    def _(step):
        for l in range(0, width, LANE):
            parts = []
            for a in range(RADIX):
                piece = pieces[a * inner // rows]
                at = pl.ds(pl.multiple_of(a * inner % rows + step * SUB, SUB), SUB)
                parts.append(
                    (
                        piece[at, l : l + LANE].astype(F32),
                        piece[at, width + l : width + l + LANE].astype(F32),
                    )
                )
            low = pl.ds(pl.multiple_of(step * SUB, SUB), SUB)
            high = pl.ds(pl.multiple_of(inner + step * SUB, SUB), SUB)
            for k, (re, im) in enumerate(radix8(parts, -1)):
                y1[k, low, l : l + LANE] = re.astype(BF)
                y1[k, high, l : l + LANE] = im.astype(BF)

    @pl.loop(0, RADIX)
    def _(k):
        z[...] = jnp.dot(f_ref[k], y1[k], preferred_element_type=F32)

        @pl.loop(0, inner // SUB)
        def _(step):
            low = pl.ds(pl.multiple_of(step * SUB, SUB), SUB)
            high = pl.ds(pl.multiple_of(inner + step * SUB, SUB), SUB)
            w = wx_ref[k, low, :] - wy_ref[...]
            size = jnp.abs(w)
            root = size * lax.rsqrt(jnp.maximum(size, 1e-30))
            onward = w > 0
            re = jnp.where(onward, horner(COS_WIDE, w), jnp.exp(-root))
            im = jnp.where(onward, root * horner(SINC_WIDE, w), 0.0)
            zr, zi = z[low, :], z[high, :]
            kb[low, :] = (zr * re - zi * im).astype(BF)
            kb[high, :] = (zr * im + zi * re).astype(BF)

        y1[k] = jnp.dot(ft_ref[k], kb[...], preferred_element_type=F32).astype(BF)

    @pl.loop(0, inner // SUB)
    def _(step):
        low = pl.ds(pl.multiple_of(step * SUB, SUB), SUB)
        high = pl.ds(pl.multiple_of(inner + step * SUB, SUB), SUB)
        for l in range(0, width, LANE):
            parts = [
                (y1[k, low, l : l + LANE].astype(F32), y1[k, high, l : l + LANE].astype(F32))
                for k in range(RADIX)
            ]
            for a, (re, im) in enumerate(radix8(parts, 1)):
                outs[a][low, l : l + LANE] = re.astype(BF)
                outs[a][low, width + l : width + l + LANE] = im.astype(BF)


def band_kernel(g_ref, off_ref, out_ref):
    rows, lanes = g_ref.shape[1], g_ref.shape[2]
    width = out_ref.shape[3]
    offset = off_ref[...]
    for part in range(2):
        x = jnp.concatenate(
            [g_ref[part].astype(F32), jnp.zeros((rows, width - lanes), F32)], axis=1
        )
        bit = 1
        while bit < width:
            x = jnp.where((offset & bit) != 0, pltpu.roll(x, bit, 1), x)
            bit *= 2
        out_ref[part, 0] = x.astype(BF)


def finish_kernel(cuts, split, cut_ref, num_ref, *refs):
    pieces = refs[:RADIX]
    f_ref, slow_in, band_ref, dx_ref, dy_ref, out_ref, z1, u, cr, ci = refs[RADIX:]
    rows, extent = slow_in.shape
    inner = extent // RADIX
    per = RADIX // cuts
    cut = cut_ref[0]
    scale = num_ref[0]
    turns = num_ref[1]
    share = num_ref[2]
    for s in range(cuts):
        for c in range(per):
            k = residue(cut, s, c, cuts, per)
            z1[k] = jnp.dot(
                pieces[s * per + c][...], f_ref[k], preferred_element_type=F32
            ).astype(BF)
    u[:, :, :PAD] = jnp.zeros((2, rows, PAD), BF)
    u[:, :, PAD + extent :] = jnp.zeros((2, rows, PAD), BF)

    @pl.loop(0, rows // SUB)
    def _(step):
        at = rows_of(step)
        for l in range(0, inner, LANE):
            parts = [
                (
                    z1[k, at, l : l + LANE].astype(F32),
                    z1[k, at, inner + l : inner + l + LANE].astype(F32),
                )
                for k in range(RADIX)
            ]
            for a, (re, im) in enumerate(radix8(parts, 1)):
                at_y = a * inner + l
                theta = scale * (slow_in[at, at_y : at_y + LANE].astype(F32) - slow_ref)
                square = theta * theta
                cosine = horner(COS_SLIM, square)
                sine = theta * horner(SINC_SLIM, square)
                u[0, at, PAD + at_y : PAD + at_y + LANE] = (re * cosine - im * sine).astype(BF)
                u[1, at, PAD + at_y : PAD + at_y + LANE] = (re * sine + im * cosine).astype(BF)

    contract = (((1,), (1,)), ((), ()))

    def mul(x, y):
        return lax.dot_general(x, y, contract, preferred_element_type=F32)

    for t in range(RADIX):
        wr = u[0, :, t * inner : t * inner + inner + 2 * PAD]
        wi = u[1, :, t * inner : t * inner + inner + 2 * PAD]
        cr[...] = mul(wr, band_ref[0, t]) - mul(wi, band_ref[1, t])
        ci[...] = mul(wr, band_ref[1, t]) + mul(wi, band_ref[0, t])

        @pl.loop(0, rows // SUB)
        def _(step):
            at = rows_of(step)
            first = t * inner
            vr = u[0, at, PAD + first : PAD + first + inner].astype(F32) + cr[at, :]
            vi = u[1, at, PAD + first : PAD + first + inner].astype(F32) + ci[at, :]
            distance = jnp.sqrt(dx_ref[at, :] + dy_ref[:, first : first + inner])
            turn = turns * distance
            theta = (turn - jnp.floor(turn + 0.5)) * (2.0 * math.pi)
            square = theta * theta
            value = (
                vr * horner(COS_WIDE, square) - vi * (theta * horner(SINC_WIDE, square))
            ) * share
            if split:
                size = out_ref.shape[2]
                for e in range(0, inner, size):
                    out_ref[(first + e) // size, at, :] = value[:, e : e + size]
            else:
                out_ref[at, first : first + inner] = value


def params():
    return pltpu.CompilerParams(vmem_limit_bytes=VMEM_LIMIT)


VMEM = pl.BlockSpec(memory_space=pltpu.VMEM)
SMEM = pl.BlockSpec(memory_space=pltpu.SMEM)


def lines_forward(field, ft, cut, cuts):
    rows, extent = field.shape[1], field.shape[2]
    inner = extent // RADIX
    tile = math.gcd(rows, 256)
    return pl.pallas_call(
        functools.partial(lines_kernel, cuts),
        grid=(rows // tile,),
        out_shape=[jax.ShapeDtypeStruct((rows, 2 * inner), BF)] * RADIX,
        in_specs=[
            SMEM,
            pl.BlockSpec((2, tile, extent), lambda i: (0, i, 0)),
            pl.BlockSpec(ft.shape, lambda i: (0, 0, 0)),
        ],
        out_specs=[pl.BlockSpec((tile, 2 * inner), lambda i: (i, 0))] * RADIX,
        scratch_shapes=[pltpu.VMEM((RADIX, tile, 2 * inner), BF)],
        compiler_params=params(),
        cost_estimate=pl.CostEstimate(
            flops=rows * RADIX * (2 * inner) ** 2 * 2,
            bytes_accessed=rows * extent * 8 + ft.size * 2,
            transcendentals=0,
        ),
        name="lines_forward",
    )(cut, field, ft)


def across(pieces, f, ft, wx, wy, cuts):
    rows = pieces[0].shape[0]
    inner = rows * cuts // RADIX
    width = pieces[0].shape[1] // 2
    return pl.pallas_call(
        functools.partial(across_kernel, cuts),
        out_shape=[jax.ShapeDtypeStruct((inner, 2 * width), BF)] * RADIX,
        in_specs=[VMEM] * (cuts + 4),
        out_specs=[VMEM] * RADIX,
        scratch_shapes=[
            pltpu.VMEM((RADIX, 2 * inner, width), BF),
            pltpu.VMEM((2 * inner, width), F32),
            pltpu.VMEM((2 * inner, width), BF),
        ],
        compiler_params=params(),
        cost_estimate=pl.CostEstimate(
            flops=2 * width * RADIX * (2 * inner) ** 2 * 2,
            bytes_accessed=24 * 1024 * 1024,
            transcendentals=0,
        ),
        name="across",
    )(*pieces, f, ft, wx, wy)


def band(rows_g, offsets, inner):
    extent = rows_g.shape[1]
    return pl.pallas_call(
        band_kernel,
        grid=(RADIX,),
        out_shape=jax.ShapeDtypeStruct((2, RADIX, inner, inner + 2 * PAD), BF),
        in_specs=[
            pl.BlockSpec((2, inner, rows_g.shape[2]), lambda t: (0, t, 0)),
            pl.BlockSpec((inner, 1), lambda t: (t, 0)),
        ],
        out_specs=pl.BlockSpec((2, 1, inner, inner + 2 * PAD), lambda t: (0, t, 0, 0)),
        compiler_params=params(),
        cost_estimate=pl.CostEstimate(
            flops=0, bytes_accessed=40 * 1024 * 1024, transcendentals=0
        ),
        name="band",
    )(rows_g, offsets)


def finish(pieces, chunk, f, slab, bands, dx, dy, cut, numbers, cuts, freqs):
    rows = pieces[0].shape[0]
    extent = slab.shape[1]
    inner = extent // RADIX
    size = extent // freqs
    split = size % LANE == 0 and inner % size == 0
    tile = math.gcd(rows, 128)
    steps = rows // tile
    if split:
        out_shape = jax.ShapeDtypeStruct((freqs, rows, size), F32)
        out_spec = pl.BlockSpec((freqs, tile, size), lambda i: (0, i, 0))
    else:
        out_shape = jax.ShapeDtypeStruct((rows, extent), F32)
        out_spec = pl.BlockSpec((tile, extent), lambda i: (i, 0))
    return pl.pallas_call(
        functools.partial(finish_kernel, cuts, split),
        grid=(steps,),
        out_shape=out_shape,
        in_specs=[SMEM, SMEM]
        + [pl.BlockSpec((tile, 2 * inner), lambda i: (i, 0))] * RADIX
        + [
            pl.BlockSpec(f.shape, lambda i: (0, 0, 0)),
            pl.BlockSpec((tile, extent), lambda i: (i + chunk * steps, 0)),
            pl.BlockSpec(bands.shape, lambda i: (0, 0, 0, 0)),
            pl.BlockSpec((tile, 1), lambda i: (i + chunk * steps, 0)),
            pl.BlockSpec((1, extent), lambda i: (0, 0)),
        ],
        out_specs=out_spec,
        scratch_shapes=[
            pltpu.VMEM((RADIX, tile, 2 * inner), BF),
            pltpu.VMEM((2, tile, extent + 2 * PAD), BF),
            pltpu.VMEM((tile, inner), F32),
            pltpu.VMEM((tile, inner), F32),
        ],
        compiler_params=params(),
        cost_estimate=pl.CostEstimate(
            flops=rows * RADIX * (2 * inner) ** 2 * 6,
            bytes_accessed=32 * 1024 * 1024,
            transcendentals=0,
        ),
        name="finish",
    )(cut, numbers, *pieces, f, slab, bands, dx, dy), split


def wave_numbers(indices, extent):
    signed = jnp.where(indices < extent // 2, indices, indices - extent)
    return signed.astype(F32) * (2.0 * math.pi / (extent * grid_step))


def back(x, axis, shift):
    count = lax.axis_size(axis)
    return lax.ppermute(x, axis, [(i, (i - shift) % count) for i in range(count)])


def forth(x, axis, shift):
    count = lax.axis_size(axis)
    return lax.ppermute(x, axis, [(i, (i + shift) % count) for i in range(count)])


def body(wavefield, slowness, block_inverse, block_lengths, slab_owner, shot_position):
    cuts = lax.axis_size("cuts")
    freqs = lax.axis_size("freq")
    rows, extent_y = wavefield.shape[2], wavefield.shape[3]
    extent_x = rows * cuts
    inner_x, inner_y = extent_x // RADIX, extent_y // RADIX
    per = RADIX // cuts
    freq_index = lax.axis_index("freq")
    cut_index = lax.axis_index("cuts")
    cut = jnp.reshape(cut_index, (1,)).astype(jnp.int32)
    hertz = band_low + band_width * (freq_index.astype(F32) + 0.5) / freqs
    angular = 2.0 * math.pi * hertz

    fy, fty = fourier_tables(extent_y)
    fy, fty = jnp.asarray(fy), jnp.asarray(fty)
    if extent_x == extent_y:
        fx, ftx = fy, fty
    else:
        fx, ftx = fourier_tables(extent_x)
        fx, ftx = jnp.asarray(fx), jnp.asarray(ftx)

    owner = slab_owner[0]
    mine = freq_index == owner
    operators = lax.psum(jnp.where(mine, block_inverse[0], jnp.zeros_like(block_inverse[0])), "freq")
    slab = lax.psum(jnp.where(mine, slowness[0], jnp.zeros_like(slowness[0])), "freq")

    spectrum = lines_forward(wavefield[0], fty, cut, cuts)

    count_x = jnp.arange(RADIX, dtype=jnp.int32)[:, None] + RADIX * jnp.arange(inner_x, dtype=jnp.int32)[None, :]
    wx = (depth_step * depth_step) * (
        (angular * slow_ref) ** 2 - wave_numbers(count_x, extent_x) ** 2
    )
    wx = wx[:, :, None]
    received = [[None] * cuts for _ in range(per)]
    for c in range(per):
        received[c][0] = spectrum[c]
        for s in range(1, cuts):
            received[c][s] = back(spectrum[s * per + c], "cuts", s)
    results = []
    for c in range(per):
        line = cut_index * per + c + RADIX * jnp.arange(inner_y, dtype=jnp.int32)
        wy = ((depth_step * depth_step) * wave_numbers(line, extent_y) ** 2)[None, :]
        results.append(across(received[c], fx, ftx, wx, wy, cuts))

    whole = [operators]
    for s in range(1, cuts):
        whole.append(back(operators, "cuts", s))
    stacked = jnp.stack(whole)
    stacked = jnp.take(stacked, (jnp.arange(cuts) - cut_index) % cuts, axis=0)
    capacity = stacked.shape[-1]
    blocks = stacked.shape[2] * cuts
    matrices = jnp.moveaxis(stacked, 0, 1).reshape(2, blocks * capacity, capacity)
    lengths = lax.dynamic_index_in_dim(block_lengths, owner, 0, keepdims=False)
    ends = jnp.cumsum(lengths)
    starts = ends - lengths
    cells = jnp.arange(extent_y, dtype=jnp.int32)
    which = jnp.sum((ends[None, :] <= cells[:, None]).astype(jnp.int32), axis=1)
    chosen = which[:, None] == jnp.arange(blocks, dtype=jnp.int32)[None, :]
    start = jnp.sum(jnp.where(chosen, starts[None, :], 0), axis=1)
    length = jnp.sum(jnp.where(chosen, lengths[None, :], 0), axis=1)
    slot = which * capacity + cells - start
    picked = jnp.take(matrices, slot, axis=1)
    picked = jnp.where(
        jnp.arange(capacity, dtype=jnp.int32)[None, None, :] < length[None, :, None], picked, 0
    ).astype(BF)
    picked = jnp.pad(picked, ((0, 0), (0, 0), (0, -capacity % LANE)))
    offsets = start - (cells // inner_y * inner_y - PAD)
    bands = band(picked, offsets[:, None].astype(jnp.int32), inner_y)

    rows_x = cut_index * rows + jnp.arange(rows, dtype=jnp.int32)
    dx = (((rows_x - shot_position[0]).astype(F32) * grid_step) ** 2)[:, None]
    dy = (((cells - shot_position[1]).astype(F32) * grid_step) ** 2 + depth_step * depth_step)[None, :]
    numbers = jnp.stack(
        [angular * depth_step, hertz * slow_ref, jnp.asarray(1.0 / math.sqrt(freqs), F32)]
    )

    chunks = rows // inner_x
    images = []
    for h in range(chunks):
        pieces = []
        for s in range(cuts):
            for c in range(per):
                x = results[c][s * chunks + h]
                pieces.append(x if s == 0 else forth(x, "cuts", s))
        part, split = finish(pieces, h, fy, slab, bands, dx, dy, cut, numbers, cuts, freqs)
        if split:
            part = lax.psum_scatter(part, "freq", scatter_dimension=0, tiled=False)
        else:
            part = lax.psum_scatter(part, "freq", scatter_dimension=1, tiled=True)
        images.append(part)
    return jnp.concatenate(images, axis=0)[None]


def solution(mesh):
    placed = (
        P("freq", None, "cuts", None),
        P("freq", "cuts", None),
        P("freq", None, "cuts", None, None),
        P(),
        P(),
        P(),
    )
    return jax.shard_map(
        body, mesh=mesh, in_specs=placed, out_specs=P(None, "cuts", "freq"), check_vma=False
    )
```

time: 965 us -> 534 us (0.55); the launches traced: 951 us -> 533 us
  local copies, waits for them, and re-layouts: 319 us -> 18.8 us
  Pallas kernels: 0 us -> 263 us
  other arithmetic: 179 us -> 16.2 us
  matrix products: 130 us -> 0 us
  blocking collectives: 98.8 us -> 0 us
    pallas_call x0 -> x10, Pallas kernels: none -> 263 us  [the longest x4 123 us: finish(): pl.pallas_call(functools.partial(finish_kernel, cuts, split), grid=(steps...]
    dot_general x12 -> x0, matrix products: 130 us -> none  [the longest x8 114 us: mixing(): jnp.einsum(formula, operand, table, preferred_element_type=jnp.float32)]
    all_gather x1 -> x0, blocking collectives: 98.8 us -> none  [body(): whole_blocks = lax.all_gather(block_inverse, 'cuts', axis=2, tiled=True)]
    all_to_all x2 -> x0, waiting for transfers between devices: 91.3 us -> none  [the longest x1 91.3 us: body(): lax.all_to_all(spectrum, 'cuts', split_axis=0, concat_axis=1, tiled=True)]
    another operation x14 -> x4, other arithmetic: 90.6 us -> 1.03 us  [the longest x1 0.56 us: body(): jnp.stack([angular * depth_step, hertz * slow_ref, jnp.asarray(1.0 / math...]
    reshape x2 -> x3, local copies, waits for them, and re-layouts: 72.4 us -> 2.14 us  [the longest x1 1.35 us: body(): jnp.moveaxis(stacked, 0, 1).reshape(2, blocks * capacity, capacity)]
    ppermute x0 -> x21, waiting for transfers between devices: none -> 63.8 us  [the longest x16 57.6 us: forth(): lax.ppermute(x, axis, [(i, (i + shift) % count) for i in range(count)])]
    unnamed x22 -> x58, local copies, waits for them, and re-layouts: 65.9 us -> 6.33 us
  transfers between devices with their start and end apart: 4 -> 26, of which waited for: 3 -> 16; matrix products, arithmetic and copies ran while one was open for 15% -> 5% of each run, Pallas kernels for 0% -> 41%
where the time goes in v1:
time: 534 us; the launch traced here: 533 us
  Pallas kernels  263 us (49%)
  waiting for transfers between devices  198 us (37%)
  starting transfers between devices  23.1 us (4%)
  local copies, waits for them, and re-layouts  18.8 us (4%)
  other arithmetic  16.2 us (3%)
  between operations  14.1 us (3%)
    pallas_call x4, Pallas kernels, finish(): pl.pallas_call(functools.partial(finish_kernel, cuts, split), grid=(steps...  123 us
    pallas_call x4, Pallas kernels, across(): pl.pallas_call(functools.partial(across_kernel, cuts), out_shape=[jax.Sha...  109 us
    reduce_scatter x4, waiting for transfers between devices, body(): part = lax.psum_scatter(part, 'freq', scatter_dimension=0, tiled=False)  87.7 us
    ppermute x16, waiting for transfers between devices, forth(): lax.ppermute(x, axis, [(i, (i + shift) % count) for i in range(count)])  57.6 us
    psum x1, waiting for transfers between devices, body(): lax.psum(jnp.where(mine, slowness[0], jnp.zeros_like(slowness[0])), 'freq')  46.6 us
    pallas_call x1, Pallas kernels, band(): pl.pallas_call(band_kernel, grid=(RADIX,), out_shape=jax.ShapeDtypeStruct...  18.5 us
    ppermute x16, starting transfers between devices, forth(): lax.ppermute(x, axis, [(i, (i + shift) % count) for i in range(count)])  16.4 us
    pallas_call x1, Pallas kernels, lines_forward(): pl.pallas_call(functools.partial(lines_kernel, cuts), grid=(rows // tile,...  12.6 us
  transfers between devices with their start and end apart: 26, of which 16 were waited for; matrix products, arithmetic and copies ran while one was open for 5% of the time, Pallas kernels for 41%

profile of v1, /device:TPU:0, one launch (start us, length us, event | category | flops | bytes accessed | tf_op | source)
XLA Modules:
  0.0 533.3 jit_solution(8949421933257229985)
XLA Ops:
  6.5 12.6 %lines_forward.1 = (bf16[1024,512]{1,0:T(8,128)(2,1)}, bf16[1024,512]{1,0:T(8,128)(2,1)}, bf16[1024,512]{1,0:T(8,128)(2,1)}, bf16[1024,512]{1,0:T(8,128)(2,1)}, ...) custom-call(s32[1]{0:T(128)} %bitcast.cut_ref, ...), custom_call_target="tpu_custom_call" | custom-call | flops 4294967296 | bytes 20971520 | tf_op jit(solution)/shard_map/lines_forward/pallas_call | solution.py:289
  40.2 6.2 %collective-permute-done.refs_1_ = bf16[1024,512]{1,0:T(8,128)(2,1)} collective-permute-done((bf16[1024,512]{1,0:T(8,128)(2,1)}, bf16[1024,512]{1,0:T(8,128)(2,1)}, u32[]{:S(2)}, u32[]{:S(2)}) %collective-permute-start) | collective-permute-done | bytes 1048608 | tf_op jit(solution)/shard_map/ppermute | solution.py:404
  46.4 27.4 %across.4 = (bf16[256,512]{1,0:T(8,128)(2,1)}, bf16[256,512]{1,0:T(8,128)(2,1)}, bf16[256,512]{1,0:T(8,128)(2,1)}, bf16[256,512]{1,0:T(8,128)(2,1)}, bf16[256,51...) custom-call(bf16[1024,512]{1,0:T(8,128)(2,1)} %get-tuple-element.45.refs_0_, ...), custom_call_target="tpu_custom_call" | custom-call | flops 2147483648 | bytes 25165824 | tf_op jit(solution)/shard_map/across/pallas_call | solution.py:314
  75.9 27.2 %across.5 = (bf16[256,512]{1,0:T(8,128)(2,1)}, bf16[256,512]{1,0:T(8,128)(2,1)}, bf16[256,512]{1,0:T(8,128)(2,1)}, bf16[256,512]{1,0:T(8,128)(2,1)}, bf16[256,51...) custom-call(bf16[1024,512]{1,0:T(8,128)(2,1)} %get-tuple-element.48.refs_0_, ...), custom_call_target="tpu_custom_call" | custom-call | flops 2147483648 | bytes 25165824 | tf_op jit(solution)/shard_map/across/pallas_call | solution.py:314
  103.3 46.6 %all-reduce.4.cloned.1.call-done = (bf16[1024,2048]{1,0:T(8,128)(2,1)}, bf16[2,20,64,64]{3,2,1,0:T(8,128)(2,1)}) async-done(((bf16[1024,2048]{1,0:T(8,128)(2,1)}, bf16[2,20,64,64]{3,2,1,0:T(8,128)(2,1)}), (bf16[1024,2048]{1,0:T(8,128)(2,1)}, bf16[2,20,64,64]{3,2,1,0:T(8,128)(2,1)})) %all-reduce.4.cloned.1.call-update) | async-done | bytes 4522000 | tf_op jit(solution)/shard_map/psum | solution.py:436
  151.4 27.3 %across.6 = (bf16[256,512]{1,0:T(8,128)(2,1)}, bf16[256,512]{1,0:T(8,128)(2,1)}, bf16[256,512]{1,0:T(8,128)(2,1)}, bf16[256,512]{1,0:T(8,128)(2,1)}, bf16[256,51...) custom-call(bf16[1024,512]{1,0:T(8,128)(2,1)} %get-tuple-element.51.refs_0_, ...), custom_call_target="tpu_custom_call" | custom-call | flops 2147483648 | bytes 25165824 | tf_op jit(solution)/shard_map/across/pallas_call | solution.py:314
  180.1 27.3 %across.7 = (bf16[256,512]{1,0:T(8,128)(2,1)}, bf16[256,512]{1,0:T(8,128)(2,1)}, bf16[256,512]{1,0:T(8,128)(2,1)}, bf16[256,512]{1,0:T(8,128)(2,1)}, bf16[256,51...) custom-call(bf16[1024,512]{1,0:T(8,128)(2,1)} %get-tuple-element.54.refs_0_, ...), custom_call_target="tpu_custom_call" | custom-call | flops 2147483648 | bytes 25165824 | tf_op jit(solution)/shard_map/across/pallas_call | solution.py:314
  211.6 7.0 %gather_fusion.1 = bf16[2048,2,64]{2,1,0:T(2,128)(2,1)S(1)} fusion(bf16[2,2560,64]{2,0,1:T(2,128)(2,1)S(1)} %bitcast.42, s32[2048]{0:T(1024)S(1)} %broadcast_clamp_fusion), kind=kCustom, calls=%fused_computation.1 | custom fusion | bytes 1056768 | tf_op jit(solution)/shard_map/jit(_take)/gather | solution.py:473
  220.5 18.5 %band.1.refs_10_ = bf16[2,8,256,512]{3,2,1,0:T(8,128)(2,1)} custom-call(bf16[2,2048,128]{2,1,0:T(8,128)(2,1)} %pad.4.g_ref, s32[2048,1]{1,0:T(8,128)} %get-tuple-element.89.off_ref), custom_call_target="tpu_custom_call" | custom-call | bytes 41943040 | tf_op jit(solution)/shard_map/band/pallas_call | solution.py:336
  239.7 30.4 %finish.7 = f32[16,256,128]{2,1,0:T(8,128)} custom-call(s32[1]{0:T(128)} %bitcast.cut_ref, f32[3]{0:T(128)} %pad_maximum_fusion.1.num_ref, bf16[256,512]{1,0:T(8,128)(2,1)} %get-tuple-element.77.refs_0_, bf16[256,512]{1,0:T(8,128)(2,1)} %get-tuple-element.78.refs_1_, bf16[256,512]{1,0:T(8,128)(2,1)} %get-tuple-element.79.refs_2_, ...), custom_call_target="tpu_custom_call" | custom-call | flops 3221225472 | bytes 33554432 | tf_op jit(solution)/shard_map/finish/pallas_call | solution.py:367
  275.1 5.2 collective-permute-done.13.refs_4_
  280.3 5.6 %collective-permute-done.14.refs_5_ = bf16[256,512]{1,0:T(8,128)(2,1)S(1)} collective-permute-done((bf16[256,512]{1,0:T(8,128)(2,1)S(1)}, bf16[256,512]{1,0:T(8,128)(2,1)S(1)}, u32[]{:S(2)}, u32[]{:S(2)}) %collective-permute-start.14) | collective-permute-done | bytes 262176 | tf_op jit(solution)/shard_map/ppermute | solution.py:409
  285.9 5.6 %collective-permute-done.15.refs_6_ = bf16[256,512]{1,0:T(8,128)(2,1)S(1)} collective-permute-done((bf16[256,512]{1,0:T(8,128)(2,1)S(1)}, bf16[256,512]{1,0:T(8,128)(2,1)S(1)}, u32[]{:S(2)}, u32[]{:S(2)}) %collective-permute-start.15) | collective-permute-done | bytes 262176 | tf_op jit(solution)/shard_map/ppermute | solution.py:409
  295.8 30.9 %finish.6 = f32[16,256,128]{2,1,0:T(8,128)} custom-call(s32[1]{0:T(128)} %bitcast.cut_ref, f32[3]{0:T(128)} %pad_maximum_fusion.1.num_ref, bf16[256,512]{1,0:T(8,128)(2,1)} %get-tuple-element.69.refs_0_, bf16[256,512]{1,0:T(8,128)(2,1)} %get-tuple-element.70.refs_1_, bf16[256,512]{1,0:T(8,128)(2,1)} %get-tuple-element.71.refs_2_, ...), custom_call_target="tpu_custom_call" | custom-call | flops 3221225472 | bytes 33554432 | tf_op jit(solution)/shard_map/finish/pallas_call | solution.py:367
  331.8 5.2 collective-permute-done.9.refs_4_
  337.0 5.6 %collective-permute-done.10.refs_5_ = bf16[256,512]{1,0:T(8,128)(2,1)S(1)} collective-permute-done((bf16[256,512]{1,0:T(8,128)(2,1)S(1)}, bf16[256,512]{1,0:T(8,128)(2,1)S(1)}, u32[]{:S(2)}, u32[]{:S(2)}) %collective-permute-start.10) | collective-permute-done | bytes 262176 | tf_op jit(solution)/shard_map/ppermute | solution.py:409
  342.6 5.5 %collective-permute-done.11.refs_6_ = bf16[256,512]{1,0:T(8,128)(2,1)S(1)} collective-permute-done((bf16[256,512]{1,0:T(8,128)(2,1)S(1)}, bf16[256,512]{1,0:T(8,128)(2,1)S(1)}, u32[]{:S(2)}, u32[]{:S(2)}) %collective-permute-start.11) | collective-permute-done | bytes 262176 | tf_op jit(solution)/shard_map/ppermute | solution.py:409
  351.6 30.5 %finish.5 = f32[16,256,128]{2,1,0:T(8,128)} custom-call(s32[1]{0:T(128)} %bitcast.cut_ref, f32[3]{0:T(128)} %pad_maximum_fusion.1.num_ref, bf16[256,512]{1,0:T(8,128)(2,1)} %get-tuple-element.61.refs_0_, bf16[256,512]{1,0:T(8,128)(2,1)} %get-tuple-element.62.refs_1_, bf16[256,512]{1,0:T(8,128)(2,1)} %get-tuple-element.63.refs_2_, ...), custom_call_target="tpu_custom_call" | custom-call | flops 3221225472 | bytes 33554432 | tf_op jit(solution)/shard_map/finish/pallas_call | solution.py:367
  387.2 5.2 collective-permute-done.4.refs_4_
  392.4 5.6 %collective-permute-done.5.refs_5_ = bf16[256,512]{1,0:T(8,128)(2,1)S(1)} collective-permute-done((bf16[256,512]{1,0:T(8,128)(2,1)S(1)}, bf16[256,512]{1,0:T(8,128)(2,1)S(1)}, u32[]{:S(2)}, u32[]{:S(2)}) %collective-permute-start.5) | collective-permute-done | bytes 262176 | tf_op jit(solution)/shard_map/ppermute | solution.py:409
  398.0 4.8 collective-permute-done.6.refs_6_
  406.3 30.7 %finish.4 = f32[16,256,128]{2,1,0:T(8,128)} custom-call(s32[1]{0:T(128)} %bitcast.cut_ref, f32[3]{0:T(128)} %pad_maximum_fusion.1.num_ref, bf16[256,512]{1,0:T(8,128)(2,1)} %get-tuple-element.47.refs_0_, bf16[256,512]{1,0:T(8,128)(2,1)} %get-tuple-element.50.refs_1_, bf16[256,512]{1,0:T(8,128)(2,1)} %get-tuple-element.53.refs_2_, ...), custom_call_target="tpu_custom_call" | custom-call | flops 3221225472 | bytes 33554432 | tf_op jit(solution)/shard_map/finish/pallas_call | solution.py:367
  437.1 23.0 %reduce-scatter.7.cloned.1.call-done = f32[1,256,128]{2,1,0:T(8,128)} async-done(((f32[16,256,128]{2,1,0:T(8,128)}), f32[1,256,128]{2,1,0:T(8,128)}) %reduce-scatter.7.cloned.1.call-update) | async-done | bytes 131088 | tf_op jit(solution)/shard_map/reduce_scatter | solution.py:498
  460.2 64.6 %reduce-scatter.5.cloned.1.call-done = f32[1,256,128]{2,1,0:T(8,128)} async-done(((f32[16,256,128]{2,1,0:T(8,128)}), f32[1,256,128]{2,1,0:T(8,128)}) %reduce-scatter.5.cloned.1.call-update) | async-done | bytes 131088 | tf_op jit(solution)/shard_map/reduce_scatter | solution.py:498
  (138 shorter events, 60.4 us)
Async XLA Ops:
  6.5 143.3 %all-reduce.4.cloned.1.call-start = ((), (), s32[]{:S(2)}) async-start(), calls=%async_computation.8 | async-start | bytes 9699328 | tf_op jit(solution)/shard_map/psum | solution.py:436
  19.1 27.3 %collective-permute-start = (bf16[1024,512]{1,0:T(8,128)(2,1)}, bf16[1024,512]{1,0:T(8,128)(2,1)}, u32[]{:S(2)}, u32[]{:S(2)}) collective-permute-start(bf16[1024,512]{1,0:T(8,128)(2,1)} %get-tuple-element.46), channel_id=1, source_target_pairs={{0,1},{1,0},{2,3},{3,2},{4,5},{5,4},{6,7},{7,6},{8,9},{9,8},{10,11... | collective-permute-start | bytes 3145736 | tf_op jit(solution)/shard_map/ppermute | solution.py:404
  22.1 53.8 %collective-permute-start.1 = (bf16[1024,512]{1,0:T(8,128)(2,1)}, bf16[1024,512]{1,0:T(8,128)(2,1)}, u32[]{:S(2)}, u32[]{:S(2)}) collective-permute-start(bf16[1024,512]{1,0:T(8,128)(2,1)} %get-tuple-element.49), channel_id=1, source_target_pairs={{0,1},{1,0},{2,3},{3,2},{4,5},{5,4},{6,7},{7,6},{8,9},{9,8},{10,11... | collective-permute-start | bytes 3145736 | tf_op jit(solution)/shard_map/ppermute | solution.py:404
  22.2 129.2 %collective-permute-start.2 = (bf16[1024,512]{1,0:T(8,128)(2,1)}, bf16[1024,512]{1,0:T(8,128)(2,1)}, u32[]{:S(2)}, u32[]{:S(2)}) collective-permute-start(bf16[1024,512]{1,0:T(8,128)(2,1)} %get-tuple-element.52), channel_id=1, source_target_pairs={{0,1},{1,0},{2,3},{3,2},{4,5},{5,4},{6,7},{7,6},{8,9},{9,8},{10,11... | collective-permute-start | bytes 3145736 | tf_op jit(solution)/shard_map/ppermute | solution.py:404
  24.1 155.1 %collective-permute-start.3 = (bf16[1024,512]{1,0:T(8,128)(2,1)}, bf16[1024,512]{1,0:T(8,128)(2,1)S(1)}, u32[]{:S(2)}, u32[]{:S(2)}) collective-permute-start(bf16[1024,512]{1,0:T(8,128)(2,1)} %get-tuple-element.55), channel_id=1, source_target_pairs={{0,1},{1,0},{2,3},{3,2},{4,5},{5,4},{6,7},{7,6},{8,9},{9,8},{10,11... | collective-permute-start | bytes 3145736 | tf_op jit(solution)/shard_map/ppermute | solution.py:404
  28.1 409.0 %reduce-scatter.11.cloned.1.call-start = ((), (), s32[]{:S(2)}) async-start(), calls=%async_computation.7 | async-start | bytes 2228224 | tf_op jit(solution)/shard_map/reduce_scatter | solution.py:498
  73.8 165.1 %collective-permute-start.17 = (bf16[256,512]{1,0:T(8,128)(2,1)}, bf16[256,512]{1,0:T(8,128)(2,1)}, u32[]{:S(2)}, u32[]{:S(2)}) collective-permute-start(bf16[256,512]{1,0:T(8,128)(2,1)} %get-tuple-element.81), channel_id=1, source_target_pairs={{0,1},{1,0},{2,3},{3,2},{4,5},{5,4},{6,7},{7,6},{8,9},{9,8},{10,11... | collective-permute-start | bytes 786440 | tf_op jit(solution)/shard_map/ppermute | solution.py:409
  103.1 135.8 %collective-permute-start.18 = (bf16[256,512]{1,0:T(8,128)(2,1)}, bf16[256,512]{1,0:T(8,128)(2,1)}, u32[]{:S(2)}, u32[]{:S(2)}) collective-permute-start(bf16[256,512]{1,0:T(8,128)(2,1)} %get-tuple-element.82), channel_id=1, source_target_pairs={{0,1},{1,0},{2,3},{3,2},{4,5},{5,4},{6,7},{7,6},{8,9},{9,8},{10,11... | collective-permute-start | bytes 786440 | tf_op jit(solution)/shard_map/ppermute | solution.py:409
  149.9 59.0 %collective-permute-start.8 = (bf16[2,20,64,64]{3,2,1,0:T(8,128)(2,1)}, bf16[2,20,64,64]{3,2,1,0:T(8,128)(2,1)S(1)}, u32[]{:S(2)}, u32[]{:S(2)}) collective-permute-start(bf16[2,20,64,64]{3,2,1,0:T(8,128)(2,1)} %get-tuple-element.88), channel_id=1, source_target_pairs={{0,1},{1,0},{2,3},{3,2},{4,5},{5,4},{6,7},{7,6},{8,9},{9,8},{10,11... | collective-permute-start | bytes 983048 | tf_op jit(solution)/shard_map/ppermute | solution.py:404
  178.6 60.3 %collective-permute-start.19 = (bf16[256,512]{1,0:T(8,128)(2,1)}, bf16[256,512]{1,0:T(8,128)(2,1)}, u32[]{:S(2)}, u32[]{:S(2)}) collective-permute-start(bf16[256,512]{1,0:T(8,128)(2,1)} %get-tuple-element.83), channel_id=1, source_target_pairs={{0,1},{1,0},{2,3},{3,2},{4,5},{5,4},{6,7},{7,6},{8,9},{9,8},{10,11... | collective-permute-start | bytes 786440 | tf_op jit(solution)/shard_map/ppermute | solution.py:409
  207.4 31.5 %collective-permute-start.20 = (bf16[256,512]{1,0:T(8,128)(2,1)}, bf16[256,512]{1,0:T(8,128)(2,1)S(1)}, u32[]{:S(2)}, u32[]{:S(2)}) collective-permute-start(bf16[256,512]{1,0:T(8,128)(2,1)} %get-tuple-element.84), channel_id=1, source_target_pairs={{0,1},{1,0},{2,3},{3,2},{4,5},{5,4},{6,7},{7,6},{8,9},{9,8},{10,11... | collective-permute-start | bytes 786440 | tf_op jit(solution)/shard_map/ppermute | solution.py:409
  270.2 166.9 %reduce-scatter.9.cloned.1.call-start = ((), (), s32[]{:S(2)}) async-start(), calls=%async_computation.6 | async-start | bytes 2228224 | tf_op jit(solution)/shard_map/reduce_scatter | solution.py:498
  271.6 14.3 %collective-permute-start.14 = (bf16[256,512]{1,0:T(8,128)(2,1)S(1)}, bf16[256,512]{1,0:T(8,128)(2,1)S(1)}, u32[]{:S(2)}, u32[]{:S(2)}) collective-permute-start(bf16[256,512]{1,0:T(8,128)(2,1)S(1)} %copy-done.26), channel_id=1, source_target_pairs={{0,1},{1,0},{2,3},{3,2},{4,5},{5,4},{6,7},{7,6},{8,9},{9,8},{10,11... | collective-permute-start | bytes 786440 | tf_op jit(solution)/shard_map/ppermute | solution.py:409
  273.1 18.4 %collective-permute-start.15 = (bf16[256,512]{1,0:T(8,128)(2,1)S(1)}, bf16[256,512]{1,0:T(8,128)(2,1)S(1)}, u32[]{:S(2)}, u32[]{:S(2)}) collective-permute-start(bf16[256,512]{1,0:T(8,128)(2,1)S(1)} %copy-done.27), channel_id=1, source_target_pairs={{0,1},{1,0},{2,3},{3,2},{4,5},{5,4},{6,7},{7,6},{8,9},{9,8},{10,11... | collective-permute-start | bytes 786440 | tf_op jit(solution)/shard_map/ppermute | solution.py:409
  273.6 21.5 %collective-permute-start.16 = (bf16[256,512]{1,0:T(8,128)(2,1)S(1)}, bf16[256,512]{1,0:T(8,128)(2,1)S(1)}, u32[]{:S(2)}, u32[]{:S(2)}) collective-permute-start(bf16[256,512]{1,0:T(8,128)(2,1)S(1)} %copy-done.28), channel_id=1, source_target_pairs={{0,1},{1,0},{2,3},{3,2},{4,5},{5,4},{6,7},{7,6},{8,9},{9,8},{10,11... | collective-permute-start | bytes 786440 | tf_op jit(solution)/shard_map/ppermute | solution.py:409
  326.8 133.3 %reduce-scatter.7.cloned.1.call-start = ((), (), s32[]{:S(2)}) async-start(), calls=%async_computation.5 | async-start | bytes 2228224 | tf_op jit(solution)/shard_map/reduce_scatter | solution.py:498
  328.3 14.2 %collective-permute-start.10 = (bf16[256,512]{1,0:T(8,128)(2,1)S(1)}, bf16[256,512]{1,0:T(8,128)(2,1)S(1)}, u32[]{:S(2)}, u32[]{:S(2)}) collective-permute-start(bf16[256,512]{1,0:T(8,128)(2,1)S(1)} %copy-done.22), channel_id=1, source_target_pairs={{0,1},{1,0},{2,3},{3,2},{4,5},{5,4},{6,7},{7,6},{8,9},{9,8},{10,11... | collective-permute-start | bytes 786440 | tf_op jit(solution)/shard_map/ppermute | solution.py:409
  329.7 18.4 %collective-permute-start.11 = (bf16[256,512]{1,0:T(8,128)(2,1)S(1)}, bf16[256,512]{1,0:T(8,128)(2,1)S(1)}, u32[]{:S(2)}, u32[]{:S(2)}) collective-permute-start(bf16[256,512]{1,0:T(8,128)(2,1)S(1)} %copy-done.23), channel_id=1, source_target_pairs={{0,1},{1,0},{2,3},{3,2},{4,5},{5,4},{6,7},{7,6},{8,9},{9,8},{10,11... | collective-permute-start | bytes 786440 | tf_op jit(solution)/shard_map/ppermute | solution.py:409
  330.4 20.6 %collective-permute-start.12 = (bf16[256,512]{1,0:T(8,128)(2,1)S(1)}, bf16[256,512]{1,0:T(8,128)(2,1)S(1)}, u32[]{:S(2)}, u32[]{:S(2)}) collective-permute-start(bf16[256,512]{1,0:T(8,128)(2,1)S(1)} %copy-done.25), channel_id=1, source_target_pairs={{0,1},{1,0},{2,3},{3,2},{4,5},{5,4},{6,7},{7,6},{8,9},{9,8},{10,11... | collective-permute-start | bytes 786440 | tf_op jit(solution)/shard_map/ppermute | solution.py:409
  382.2 142.6 %reduce-scatter.5.cloned.1.call-start = ((), (), s32[]{:S(2)}) async-start(), calls=%async_computation.4 | async-start | bytes 2228224 | tf_op jit(solution)/shard_map/reduce_scatter | solution.py:498
  383.1 9.2 %collective-permute-start.4 = (bf16[256,512]{1,0:T(8,128)(2,1)S(1)}, bf16[256,512]{1,0:T(8,128)(2,1)S(1)}, u32[]{:S(2)}, u32[]{:S(2)}) collective-permute-start(bf16[256,512]{1,0:T(8,128)(2,1)S(1)} %copy-done.17), channel_id=1, source_target_pairs={{0,1},{1,0},{2,3},{3,2},{4,5},{5,4},{6,7},{7,6},{8,9},{9,8},{10,11... | collective-permute-start | bytes 786440 | tf_op jit(solution)/shard_map/ppermute | solution.py:409
  383.5 14.5 %collective-permute-start.5 = (bf16[256,512]{1,0:T(8,128)(2,1)S(1)}, bf16[256,512]{1,0:T(8,128)(2,1)S(1)}, u32[]{:S(2)}, u32[]{:S(2)}) collective-permute-start(bf16[256,512]{1,0:T(8,128)(2,1)S(1)} %copy-done.18), channel_id=1, source_target_pairs={{0,1},{1,0},{2,3},{3,2},{4,5},{5,4},{6,7},{7,6},{8,9},{9,8},{10,11... | collective-permute-start | bytes 786440 | tf_op jit(solution)/shard_map/ppermute | solution.py:409
  385.1 17.6 %collective-permute-start.6 = (bf16[256,512]{1,0:T(8,128)(2,1)S(1)}, bf16[256,512]{1,0:T(8,128)(2,1)S(1)}, u32[]{:S(2)}, u32[]{:S(2)}) collective-permute-start(bf16[256,512]{1,0:T(8,128)(2,1)S(1)} %copy-done.19), channel_id=1, source_target_pairs={{0,1},{1,0},{2,3},{3,2},{4,5},{5,4},{6,7},{7,6},{8,9},{9,8},{10,11... | collective-permute-start | bytes 786440 | tf_op jit(solution)/shard_map/ppermute | solution.py:409
  385.6 20.0 %collective-permute-start.7 = (bf16[256,512]{1,0:T(8,128)(2,1)S(1)}, bf16[256,512]{1,0:T(8,128)(2,1)S(1)}, u32[]{:S(2)}, u32[]{:S(2)}) collective-permute-start(bf16[256,512]{1,0:T(8,128)(2,1)S(1)} %copy-done.21), channel_id=1, source_target_pairs={{0,1},{1,0},{2,3},{3,2},{4,5},{5,4},{6,7},{7,6},{8,9},{9,8},{10,11... | collective-permute-start | bytes 786440 | tf_op jit(solution)/shard_map/ppermute | solution.py:409
  (31 other events, 159.8 us)
Sparse Core Ops, SparseCore 0:
  28.2 121.5 all-reduce.3
  270.3 60.7 reduce-scatter.10
  335.3 60.6 reduce-scatter.8
  399.6 60.5 reduce-scatter.6
  464.2 60.5 reduce-scatter.4

commit v2 on v1

--- a/solution.py
+++ b/solution.py
@@ -184,8 +184,10 @@
                 for k in range(RADIX)
             ]
             for a, (re, im) in enumerate(radix8(parts, 1)):
-                outs[a][low, l : l + LANE] = re.astype(BF)
-                outs[a][low, width + l : width + l + LANE] = im.astype(BF)
+                out = outs[a * inner // rows]
+                at = pl.ds(pl.multiple_of(a * inner % rows + step * SUB, SUB), SUB)
+                out[at, l : l + LANE] = re.astype(BF)
+                out[at, width + l : width + l + LANE] = im.astype(BF)
 
 
 def band_kernel(g_ref, off_ref, out_ref):
@@ -313,9 +315,9 @@
     width = pieces[0].shape[1] // 2
     return pl.pallas_call(
         functools.partial(across_kernel, cuts),
-        out_shape=[jax.ShapeDtypeStruct((inner, 2 * width), BF)] * RADIX,
+        out_shape=[jax.ShapeDtypeStruct((rows, 2 * width), BF)] * cuts,
         in_specs=[VMEM] * (cuts + 4),
-        out_specs=[VMEM] * RADIX,
+        out_specs=[VMEM] * cuts,
         scratch_shapes=[
             pltpu.VMEM((RADIX, 2 * inner, width), BF),
             pltpu.VMEM((2 * inner, width), F32),
@@ -350,8 +352,8 @@
     )(rows_g, offsets)
 
 
-def finish(pieces, chunk, f, slab, bands, dx, dy, cut, numbers, cuts, freqs):
-    rows = pieces[0].shape[0]
+def finish(pieces, chunk, chunks, f, slab, bands, dx, dy, cut, numbers, cuts, freqs):
+    rows = pieces[0].shape[0] // chunks
     extent = slab.shape[1]
     inner = extent // RADIX
     size = extent // freqs
@@ -369,7 +371,7 @@
         grid=(steps,),
         out_shape=out_shape,
         in_specs=[SMEM, SMEM]
-        + [pl.BlockSpec((tile, 2 * inner), lambda i: (i, 0))] * RADIX
+        + [pl.BlockSpec((tile, 2 * inner), lambda i: (i + chunk * steps, 0))] * RADIX
         + [
             pl.BlockSpec(f.shape, lambda i: (0, 0, 0)),
             pl.BlockSpec((tile, extent), lambda i: (i + chunk * steps, 0)),
@@ -453,6 +455,7 @@
         wy = ((depth_step * depth_step) * wave_numbers(line, extent_y) ** 2)[None, :]
         results.append(across(received[c], fx, ftx, wx, wy, cuts))
 
+    operators, slab, _ = lax.optimization_barrier((operators, slab, results[-1][0]))
     whole = [operators]
     for s in range(1, cuts):
         whole.append(back(operators, "cuts", s))
@@ -485,15 +488,14 @@
         [angular * depth_step, hertz * slow_ref, jnp.asarray(1.0 / math.sqrt(freqs), F32)]
     )
 
-    chunks = rows // inner_x
+    chunks = 2
+    pieces = []
+    for s in range(cuts):
+        for c in range(per):
+            pieces.append(results[c][s] if s == 0 else forth(results[c][s], "cuts", s))
     images = []
     for h in range(chunks):
-        pieces = []
-        for s in range(cuts):
-            for c in range(per):
-                x = results[c][s * chunks + h]
-                pieces.append(x if s == 0 else forth(x, "cuts", s))
-        part, split = finish(pieces, h, fy, slab, bands, dx, dy, cut, numbers, cuts, freqs)
+        part, split = finish(pieces, h, chunks, fy, slab, bands, dx, dy, cut, numbers, cuts, freqs)
         if split:
             part = lax.psum_scatter(part, "freq", scatter_dimension=0, tiled=False)
         else:

time: 534 us -> 452 us (0.85)
  waiting for transfers between devices: 198 us -> 145 us
  starting transfers between devices: 23.1 us -> 10.8 us
  Pallas kernels: 263 us -> 252 us
    ppermute x16 -> x4, waiting for transfers between devices: 57.6 us -> 0.01 us  [forth(): lax.ppermute(x, axis, [(i, (i + shift) % count) for i in range(count)])]
    ppermute x16 -> x4, starting transfers between devices: 16.4 us -> 4.22 us  [forth(): lax.ppermute(x, axis, [(i, (i + shift) % count) for i in range(count)])]
    pallas_call x4 -> x2, Pallas kernels: 123 us -> 112 us  [finish(): pl.pallas_call(functools.partial(finish_kernel, cuts, split), grid=(steps...]
    reduce_scatter x4 -> x2, waiting for transfers between devices: 87.7 us -> 91.8 us  [body(): part = lax.psum_scatter(part, 'freq', scatter_dimension=0, tiled=False)]
  transfers between devices with their start and end apart: 26 -> 12, of which waited for: 16 -> 4; matrix products, arithmetic and copies ran while one was open for 5% -> 6% of each run, Pallas kernels for 41% -> 41%
where the time goes in v2:
time: 452 us
  Pallas kernels  252 us (56%)
  waiting for transfers between devices  145 us (32%)
  other arithmetic  16.4 us (4%)
  between operations  13.9 us (3%)
  local copies, waits for them, and re-layouts  13.6 us (3%)
  starting transfers between devices  10.8 us (2%)
    pallas_call x2, Pallas kernels, finish(): pl.pallas_call(functools.partial(finish_kernel, cuts, split), grid=(steps...  112 us
    pallas_call x4, Pallas kernels, across(): pl.pallas_call(functools.partial(across_kernel, cuts), out_shape=[jax.Sha...  109 us
    reduce_scatter x2, waiting for transfers between devices, body(): part = lax.psum_scatter(part, 'freq', scatter_dimension=0, tiled=False)  91.8 us
    psum x1, waiting for transfers between devices, body(): lax.psum(jnp.where(mine, block_inverse[0], jnp.zeros_like(block_inverse[0...  46.4 us
    pallas_call x1, Pallas kernels, band(): pl.pallas_call(band_kernel, grid=(RADIX,), out_shape=jax.ShapeDtypeStruct...  18.4 us
    pallas_call x1, Pallas kernels, lines_forward(): pl.pallas_call(functools.partial(lines_kernel, cuts), grid=(rows // tile,...  12.6 us
  transfers between devices with their start and end apart: 12, of which 4 were waited for; matrix products, arithmetic and copies ran while one was open for 6% of the time, Pallas kernels for 41%

profile of v2, /device:TPU:0, one launch (start us, length us, event | category | flops | bytes accessed | tf_op | source)
XLA Modules:
  0.0 451.6 jit_solution(11646264798155107904)
XLA Ops:
  6.5 12.6 %lines_forward.1 = (bf16[1024,512]{1,0:T(8,128)(2,1)}, bf16[1024,512]{1,0:T(8,128)(2,1)}, bf16[1024,512]{1,0:T(8,128)(2,1)}, bf16[1024,512]{1,0:T(8,128)(2,1)}, ...) custom-call(s32[1]{0:T(128)} %bitcast.cut_ref, ...), custom_call_target="tpu_custom_call" | custom-call | flops 4294967296 | bytes 20971520 | tf_op jit(solution)/shard_map/lines_forward/pallas_call | solution.py:291
  19.1 3.0 collective-permute-start.3
  22.2 2.0 collective-permute-start.1
  24.9 2.3 select_bitcast_fusion
  32.1 1.5 fusion.2
  34.1 1.4 fusion.9.refs_4_
  36.8 1.5 multiply_multiply_fusion.refs_11_
  40.0 6.5 %collective-permute-done.3.refs_1_ = bf16[1024,512]{1,0:T(8,128)(2,1)} collective-permute-done((bf16[1024,512]{1,0:T(8,128)(2,1)}, bf16[1024,512]{1,0:T(8,128)(2,1)}, u32[]{:S(2)}, u32[]{:S(2)}) %collective-permute-start.3) | collective-permute-done | bytes 1048608 | tf_op jit(solution)/shard_map/ppermute | solution.py:406
  46.4 27.4 %across.7 = (bf16[1024,512]{1,0:T(8,128)(2,1)}, bf16[1024,512]{1,0:T(8,128)(2,1)}) custom-call(bf16[1024,512]{1,0:T(8,128)(2,1)} %get-tuple-element.32.refs_0_, bf16[1024,512]{1,0:T(8,128)(2,1)} %collective-permute-done.3.refs_1_, bf16[8,512,512]{2,1,0:T(8,128)(2,1)} %constant.141.clone.refs_2_.refs_8_, bf16[8,512,512]{2,1,0:T(8,128)(2,1)} %constant.142.clone.ft_ref.refs_3_, ...), custom_call_target="tpu_custom_call" | custom-call | flops 2147483648 | bytes 25165824 | tf_op jit(solution)/shard_map/across/pallas_call | solution.py:316
  73.8 2.1 collective-permute-start.7
  75.9 27.3 %across.6 = (bf16[1024,512]{1,0:T(8,128)(2,1)}, bf16[1024,512]{1,0:T(8,128)(2,1)}) custom-call(bf16[1024,512]{1,0:T(8,128)(2,1)} %get-tuple-element.29.refs_0_, bf16[1024,512]{1,0:T(8,128)(2,1)} %collective-permute-done.2.refs_1_, bf16[8,512,512]{2,1,0:T(8,128)(2,1)} %constant.141.clone.refs_2_.refs_8_, bf16[8,512,512]{2,1,0:T(8,128)(2,1)} %constant.142.clone.ft_ref.refs_3_, ...), custom_call_target="tpu_custom_call" | custom-call | flops 2147483648 | bytes 25165824 | tf_op jit(solution)/shard_map/across/pallas_call | solution.py:316
  103.3 46.4 %all-reduce.4.cloned.1.call-done = (bf16[2,20,64,64]{3,2,1,0:T(8,128)(2,1)}, bf16[1024,2048]{1,0:T(8,128)(2,1)}) async-done(((bf16[2,20,64,64]{3,2,1,0:T(8,128)(2,1)}, bf16[1024,2048]{1,0:T(8,128)(2,1)}), (bf16[2,20,64,64]{3,2,1,0:T(8,128)(2,1)}, bf16[1024,2048]{1,0:T(8,128)(2,1)})) %all-reduce.4.cloned.1.call-update) | async-done | bytes 4522000 | tf_op jit(solution)/shard_map/psum | solution.py:437
  149.8 1.5 collective-permute-start.8
  151.2 27.3 %across.5 = (bf16[1024,512]{1,0:T(8,128)(2,1)}, bf16[1024,512]{1,0:T(8,128)(2,1)}) custom-call(bf16[1024,512]{1,0:T(8,128)(2,1)} %get-tuple-element.26.refs_0_, bf16[1024,512]{1,0:T(8,128)(2,1)} %collective-permute-done.1.refs_1_, bf16[8,512,512]{2,1,0:T(8,128)(2,1)} %constant.141.clone.refs_2_.refs_8_, bf16[8,512,512]{2,1,0:T(8,128)(2,1)} %constant.142.clone.ft_ref.refs_3_, ...), custom_call_target="tpu_custom_call" | custom-call | flops 2147483648 | bytes 25165824 | tf_op jit(solution)/shard_map/across/pallas_call | solution.py:316
  180.1 27.3 %across.4 = (bf16[1024,512]{1,0:T(8,128)(2,1)}, bf16[1024,512]{1,0:T(8,128)(2,1)}) custom-call(bf16[1024,512]{1,0:T(8,128)(2,1)} %get-tuple-element.23.refs_0_, bf16[1024,512]{1,0:T(8,128)(2,1)} %copy-done, bf16[8,512,512]{2,1,0:T(8,128)(2,1)} %constant.141.clone.refs_2_.refs_8_, bf16[8,512,512]{2,1,0:T(8,128)(2,1)} %constant.142.clone.ft_ref.refs_3_, ...), custom_call_target="tpu_custom_call" | custom-call | flops 2147483648 | bytes 25165824 | tf_op jit(solution)/shard_map/across/pallas_call | solution.py:316
  207.4 1.5 collective-permute-start.4
  210.8 1.4 copy.33
  212.1 7.0 %gather_fusion.1 = bf16[2048,2,64]{2,1,0:T(2,128)(2,1)S(1)} fusion(bf16[2,2560,64]{2,0,1:T(2,128)(2,1)S(1)} %bitcast.40, s32[2048]{0:T(1024)S(1)} %broadcast_clamp_fusion), kind=kCustom, calls=%fused_computation.1 | custom fusion | bytes 1056768 | tf_op jit(solution)/shard_map/jit(_take)/gather | solution.py:476
  221.1 18.4 %band.1.refs_10_ = bf16[2,8,256,512]{3,2,1,0:T(8,128)(2,1)} custom-call(bf16[2,2048,128]{2,1,0:T(8,128)(2,1)} %pad.4.g_ref, s32[2048,1]{1,0:T(8,128)} %get-tuple-element.45.off_ref), custom_call_target="tpu_custom_call" | custom-call | bytes 41943040 | tf_op jit(solution)/shard_map/band/pallas_call | solution.py:338
  239.5 55.8 %finish.2 = f32[16,512,128]{2,1,0:T(8,128)} custom-call(s32[1]{0:T(128)} %bitcast.cut_ref, f32[3]{0:T(128)} %pad_maximum_fusion.1.num_ref, bf16[1024,512]{1,0:T(8,128)(2,1)} %get-tuple-element.25.refs_0_, bf16[1024,512]{1,0:T(8,128)(2,1)} %get-tuple-element.28.refs_1_, bf16[1024,512]{1,0:T(8,128)(2,1)} %get-tuple-element.31.refs_2_, ...), custom_call_target="tpu_custom_call" | custom-call | flops 6442450944 | bytes 33554432 | tf_op jit(solution)/shard_map/finish/pallas_call | solution.py:369
  295.4 56.0 %finish.3 = f32[16,512,128]{2,1,0:T(8,128)} custom-call(s32[1]{0:T(128)} %bitcast.cut_ref, f32[3]{0:T(128)} %pad_maximum_fusion.1.num_ref, bf16[1024,512]{1,0:T(8,128)(2,1)} %get-tuple-element.25.refs_0_, bf16[1024,512]{1,0:T(8,128)(2,1)} %get-tuple-element.28.refs_1_, bf16[1024,512]{1,0:T(8,128)(2,1)} %get-tuple-element.31.refs_2_, ...), custom_call_target="tpu_custom_call" | custom-call | flops 6442450944 | bytes 33554432 | tf_op jit(solution)/shard_map/finish/pallas_call | solution.py:369
  351.5 15.7 %reduce-scatter.3.cloned.1.call-done = f32[1,512,128]{2,1,0:T(8,128)} async-done(((f32[16,512,128]{2,1,0:T(8,128)}), f32[1,512,128]{2,1,0:T(8,128)}) %reduce-scatter.3.cloned.1.call-update) | async-done | bytes 262160 | tf_op jit(solution)/shard_map/reduce_scatter | solution.py:500
  367.2 76.1 %reduce-scatter.5.cloned.1.call-done = f32[1,512,128]{2,1,0:T(8,128)} async-done(((f32[16,512,128]{2,1,0:T(8,128)}), f32[1,512,128]{2,1,0:T(8,128)}) %reduce-scatter.5.cloned.1.call-update) | async-done | bytes 262160 | tf_op jit(solution)/shard_map/reduce_scatter | solution.py:500
  443.2 1.9 maximum_bitcast_fusion
  (56 shorter events, 14.0 us)
Async XLA Ops:
  6.5 143.2 %all-reduce.4.cloned.1.call-start = ((), (), s32[]{:S(2)}) async-start(), calls=%async_computation.4 | async-start | bytes 9699328 | tf_op jit(solution)/shard_map/psum | solution.py:437
  19.1 27.3 %collective-permute-start.3 = (bf16[1024,512]{1,0:T(8,128)(2,1)}, bf16[1024,512]{1,0:T(8,128)(2,1)}, u32[]{:S(2)}, u32[]{:S(2)}) collective-permute-start(bf16[1024,512]{1,0:T(8,128)(2,1)} %get-tuple-element.33), channel_id=1, source_target_pairs={{0,1},{1,0},{2,3},{3,2},{4,5},{5,4},{6,7},{7,6},{8,9},{9,8},{10,11... | collective-permute-start | bytes 3145736 | tf_op jit(solution)/shard_map/ppermute | solution.py:406
  22.1 53.8 %collective-permute-start.2 = (bf16[1024,512]{1,0:T(8,128)(2,1)}, bf16[1024,512]{1,0:T(8,128)(2,1)}, u32[]{:S(2)}, u32[]{:S(2)}) collective-permute-start(bf16[1024,512]{1,0:T(8,128)(2,1)} %get-tuple-element.30), channel_id=1, source_target_pairs={{0,1},{1,0},{2,3},{3,2},{4,5},{5,4},{6,7},{7,6},{8,9},{9,8},{10,11... | collective-permute-start | bytes 3145736 | tf_op jit(solution)/shard_map/ppermute | solution.py:406
  22.2 129.1 %collective-permute-start.1 = (bf16[1024,512]{1,0:T(8,128)(2,1)}, bf16[1024,512]{1,0:T(8,128)(2,1)}, u32[]{:S(2)}, u32[]{:S(2)}) collective-permute-start(bf16[1024,512]{1,0:T(8,128)(2,1)} %get-tuple-element.27), channel_id=1, source_target_pairs={{0,1},{1,0},{2,3},{3,2},{4,5},{5,4},{6,7},{7,6},{8,9},{9,8},{10,11... | collective-permute-start | bytes 3145736 | tf_op jit(solution)/shard_map/ppermute | solution.py:406
  24.1 155.0 %collective-permute-start = (bf16[1024,512]{1,0:T(8,128)(2,1)}, bf16[1024,512]{1,0:T(8,128)(2,1)S(1)}, u32[]{:S(2)}, u32[]{:S(2)}) collective-permute-start(bf16[1024,512]{1,0:T(8,128)(2,1)} %get-tuple-element.24), channel_id=1, source_target_pairs={{0,1},{1,0},{2,3},{3,2},{4,5},{5,4},{6,7},{7,6},{8,9},{9,8},{10,11... | collective-permute-start | bytes 3145736 | tf_op jit(solution)/shard_map/ppermute | solution.py:406
  24.9 2.3 copy-start.2
  28.0 339.1 %reduce-scatter.3.cloned.1.call-start = ((), (), s32[]{:S(2)}) async-start(), calls=%async_computation.2 | async-start | bytes 4456448 | tf_op jit(solution)/shard_map/reduce_scatter | solution.py:500
  32.0 4.1 copy-start.3
  73.8 165.7 %collective-permute-start.7 = (bf16[1024,512]{1,0:T(8,128)(2,1)}, bf16[1024,512]{1,0:T(8,128)(2,1)}, u32[]{:S(2)}, u32[]{:S(2)}) collective-permute-start(bf16[1024,512]{1,0:T(8,128)(2,1)} %get-tuple-element.38), channel_id=1, source_target_pairs={{0,1},{1,0},{2,3},{3,2},{4,5},{5,4},{6,7},{7,6},{8,9},{9,8},{10,11... | collective-permute-start | bytes 3145736 | tf_op jit(solution)/shard_map/ppermute | solution.py:411
  103.2 136.3 %collective-permute-start.6 = (bf16[1024,512]{1,0:T(8,128)(2,1)}, bf16[1024,512]{1,0:T(8,128)(2,1)}, u32[]{:S(2)}, u32[]{:S(2)}) collective-permute-start(bf16[1024,512]{1,0:T(8,128)(2,1)} %get-tuple-element.37), channel_id=1, source_target_pairs={{0,1},{1,0},{2,3},{3,2},{4,5},{5,4},{6,7},{7,6},{8,9},{9,8},{10,11... | collective-permute-start | bytes 3145736 | tf_op jit(solution)/shard_map/ppermute | solution.py:411
  149.8 59.7 %collective-permute-start.8 = (bf16[2,20,64,64]{3,2,1,0:T(8,128)(2,1)}, bf16[2,20,64,64]{3,2,1,0:T(8,128)(2,1)S(1)}, u32[]{:S(2)}, u32[]{:S(2)}) collective-permute-start(bf16[2,20,64,64]{3,2,1,0:T(8,128)(2,1)} %get-tuple-element.40), channel_id=1, source_target_pairs={{0,1},{1,0},{2,3},{3,2},{4,5},{5,4},{6,7},{7,6},{8,9},{9,8},{10,11... | collective-permute-start | bytes 983048 | tf_op jit(solution)/shard_map/ppermute | solution.py:406
  178.5 61.0 %collective-permute-start.5 = (bf16[1024,512]{1,0:T(8,128)(2,1)}, bf16[1024,512]{1,0:T(8,128)(2,1)}, u32[]{:S(2)}, u32[]{:S(2)}) collective-permute-start(bf16[1024,512]{1,0:T(8,128)(2,1)} %get-tuple-element.36), channel_id=1, source_target_pairs={{0,1},{1,0},{2,3},{3,2},{4,5},{5,4},{6,7},{7,6},{8,9},{9,8},{10,11... | collective-permute-start | bytes 3145736 | tf_op jit(solution)/shard_map/ppermute | solution.py:411
  179.1 1.0 copy-start
  180.1 29.4 %copy-start.1 = (bf16[2,20,64,64]{3,2,1,0:T(8,128)(2,1)S(1)}, bf16[2,20,64,64]{3,2,1,0:T(8,128)(2,1)}, u32[]{:S(2)}) copy-start(bf16[2,20,64,64]{3,2,1,0:T(8,128)(2,1)} %get-tuple-element.40) | copy-start | bytes 983044
  207.4 32.2 %collective-permute-start.4 = (bf16[1024,512]{1,0:T(8,128)(2,1)}, bf16[1024,512]{1,0:T(8,128)(2,1)}, u32[]{:S(2)}, u32[]{:S(2)}) collective-permute-start(bf16[1024,512]{1,0:T(8,128)(2,1)} %get-tuple-element.35), channel_id=1, source_target_pairs={{0,1},{1,0},{2,3},{3,2},{4,5},{5,4},{6,7},{7,6},{8,9},{9,8},{10,11... | collective-permute-start | bytes 3145736 | tf_op jit(solution)/shard_map/ppermute | solution.py:411
  295.3 147.9 %reduce-scatter.5.cloned.1.call-start = ((), (), s32[]{:S(2)}) async-start(), calls=%async_computation.3 | async-start | bytes 4456448 | tf_op jit(solution)/shard_map/reduce_scatter | solution.py:500
Sparse Core Ops, SparseCore 0:
  28.2 121.5 all-reduce.3
  295.5 71.6 reduce-scatter.2
  371.5 71.6 reduce-scatter.4
